TPU v7x, 32 devices: a whole 2x2x4 slice. The times are simulated.
32 devices in a mesh: img: 8 (over z, y), row: 4 (over x, core).
Axes of the slice: x: 2, y: 2, z: 4, core: 2. Of those that a mesh axis runs over, the one named last changes fastest.
Arguments:
- images: bfloat16 [24, 32, 32, 384], P('img', 'row'), may hold values from -8 to 8
- level_count: int32 [24], P('img'), may hold values from 2 to 1280
- level_index: int32 [24], P('img'), may hold values from 0 to 1278, as said below
- labels: int32 [24], P('img'), may hold values from 0 to 999
- first_gain: bfloat16 [384], replicated, may hold values from 0.5 to 1.5
- first_shift: bfloat16 [384], replicated, may hold values from -1.75 to 1.75
- first_kernel: bfloat16 [3456, 384], replicated, may hold values from -0.109375 to 0.109375
- first_offset: bfloat16 [384], replicated, may hold values from -1.75 to 1.75
- embed_weight: bfloat16 [768, 768], replicated, may hold values from -0.21875 to 0.21875
- embed_offset: bfloat16 [768], replicated, may hold values from -1.75 to 1.75
- class_table: bfloat16 [1000, 768], replicated, may hold values from -6 to 6
- second_gain: bfloat16 [384], replicated, may hold values from 0.5 to 1.5
- second_shift: bfloat16 [384], replicated, may hold values from -1.75 to 1.75
- second_kernel: bfloat16 [3456, 384], replicated, may hold values from -0.109375 to 0.109375
- second_offset: bfloat16 [384], replicated, may hold values from -1.75 to 1.75
- third_gain: bfloat16 [384], replicated, may hold values from 0.5 to 1.5
- third_shift: bfloat16 [384], replicated, may hold values from -1.75 to 1.75
- joint_weight: bfloat16 [384, 1152], replicated, may hold values from -0.3125 to 0.3125
- joint_offset: bfloat16 [768], replicated, may hold values from -1.75 to 1.75
- output_weight: bfloat16 [384, 384], replicated, may hold values from -2.5 to 2.5
- output_offset: bfloat16 [384], replicated, may hold values from -1.75 to 1.75
- cotangent: bfloat16 [24, 32, 32, 384], P('img', 'row'), may hold values from -8 to 8
Outputs:
- result: bfloat16 [24, 32, 32, 384], P('img', 'row')
- images_gradient: float32 [24, 32, 32, 384], P('img', 'row')
- first_gain_gradient: float32 [384], P('row')
- first_shift_gradient: float32 [384], P('row')
- first_kernel_gradient: float32 [3456, 384], P('row')
- first_offset_gradient: float32 [384], P('row')
- embed_weight_gradient: float32 [768, 768], P('row')
- embed_offset_gradient: float32 [768], P('row')
- class_table_gradient: float32 [1000, 768], P('row')
- second_gain_gradient: float32 [384], P('row')
- second_shift_gradient: float32 [384], P('row')
- second_kernel_gradient: float32 [3456, 384], P('row')
- second_offset_gradient: float32 [384], P('row')
- third_gain_gradient: float32 [384], P('row')
- third_shift_gradient: float32 [384], P('row')
- joint_weight_gradient: float32 [384, 1152], P('row')
- joint_offset_gradient: float32 [768], P('row')
- output_weight_gradient: float32 [384, 384], P('row')
- output_offset_gradient: float32 [384], P('row')
Inputs may be any that keep to these rules, and one draw needn't show every extreme that they name: Each image's level_index is below its level_count - 1.
All inputs are finite; a program needn't handle non-finite values.
Results may differ from a plain program's by a relative error of at most 0.017.
Values may be sent and summed in bfloat16 or wider, within the bound.
A program may use at most 192 MiB of HBM per device.

v0:
```python
import math

import jax
import jax.numpy as jnp
from jax import lax
from jax.experimental import pallas as pl
from jax.experimental.pallas import tpu as pltpu
from jax.sharding import PartitionSpec as P

GROUPS = 32
HEAD = 64
MESH = pl.DeviceIdType.MESH

norm_eps = 1e-05
sigma_least = 0.002
sigma_most = 80.0
sigma_power = 7.0
float_type = jnp.float32
low_type = jnp.bfloat16
contract_cols = (((1,), (1,)), ((), ()))


def peers():
    i = lax.axis_index("img")
    r = lax.axis_index("row")
    c = lax.rem(r, 2)
    near = r + 1 - 2 * c
    return (i, r, c, {1: (i, near), 2: (i, lax.rem(r + 2, 4)), 3: (i, 3 - r)})


def half_silu(v):
    h = 0.5 * v
    return h * jnp.tanh(h) + h


def fill_row(buf, start, act, channels, width):
    col = lax.broadcasted_iota(jnp.int32, (width, channels), 0)
    left = jnp.where(col == 0, 0.0, pltpu.roll(act, 1, 0))
    right = jnp.where(col == width - 1, 0.0, pltpu.roll(act, width - 1, 0))
    rows = pl.ds(start, width)
    buf[rows, 0:channels] = left.astype(low_type)
    buf[rows, channels : 2 * channels] = act.astype(low_type)
    buf[rows, 2 * channels : 3 * channels] = right.astype(low_type)


def pack_stats(first, second):
    channels = first.shape[1]
    row = lax.broadcasted_iota(jnp.int32, (8, channels), 0)

    def terms(v):
        a = v.astype(low_type).astype(float_type)
        b = (v - a).astype(low_type).astype(float_type)
        c = v - a - b
        return jnp.where(row == 0, a, jnp.where(row == 1, b, jnp.where(row == 2, c, 0.0)))

    return jnp.concatenate([terms(first), terms(second)], axis=0).astype(low_type)


def block_ones(channels, per):
    a = lax.broadcasted_iota(jnp.int32, (channels, channels), 0)
    b = lax.broadcasted_iota(jnp.int32, (channels, channels), 1)
    a = lax.shift_right_logical(a * 43691, 19)
    b = lax.shift_right_logical(b * 43691, 19)
    return jnp.where(a == b, 1.0, 0.0).astype(low_type)


def combine_stats(parts, ones, entries):
    total = jnp.dot(jnp.concatenate(parts, axis=0), ones, preferred_element_type=float_type)
    first = total[0:8] + total[16:24] + total[32:40] + total[48:56]
    second = total[8:16] + total[24:32] + total[40:48] + total[56:64]
    first = jnp.sum(first, axis=0, keepdims=True) * (1.0 / entries)
    second = jnp.sum(second, axis=0, keepdims=True) * (1.0 / entries)
    return first, second


def chip_peers(i, r):
    size = lax.axis_size("img")
    z = lax.rem(lax.div(i, 2), 4)
    e = lax.div(i, 8)
    others = (z + 1 - 2 * lax.rem(z, 2), lax.rem(z + 2, 4), 3 - z)
    more = size // 8
    return {
        "y": [(i + 1 - 2 * lax.rem(i, 2), r)],
        "z": [(i + 2 * (n - z), r) for n in others],
        "e": [(i + 8 * (lax.rem(e + k, more) - e), r) for k in range(1, more)],
        "at": (lax.rem(i, 2), z),
        "pieces": others,
    }


class Reduction:
    def __init__(self, out, lanes, n, q, refs, who, place, cs, cr, es, er):
        if n is not None:
            refs = (refs[0].at[n],) + tuple(ref.at[n] for ref in refs[1:])
        self.grad, self.got_core, self.got_x, self.own, self.got_y, self.got_z, self.got_e = refs
        self.out, self.lanes, self.q, self.who = out, lanes, q, who
        self.c, self.x, self.chips = place
        self.y, self.z = self.chips["at"]
        self.sems = (cs, cr, es, er)
        self.size = self.got_x.shape[0]

    def copy(self, src, dst, n, at, extra=False):
        send, recv = self.sems[2:] if extra else self.sems[:2]
        return pltpu.make_async_remote_copy(
            src, dst, send.at[self.q, n], recv.at[self.q, n], device_id=at, device_id_type=MESH
        )

    def half(self, y):
        size = self.size // 2
        return pl.ds(pl.multiple_of(y * size, size), size)

    def piece(self, z, y=0):
        size = self.size // 8
        return pl.ds(pl.multiple_of(y * (self.size // 2) + z * size, size), size)

    def core_copies(self):
        return [
            self.copy(self.grad.at[2 * n + 1 - self.c], self.got_core.at[n], n, self.who[1])
            for n in range(2)
        ]

    def x_copies(self):
        return [self.copy(self.grad.at[2 * (1 - self.x) + self.c], self.got_x, 2, self.who[2])]

    def y_copies(self):
        return [self.copy(self.got_x.at[self.half(1 - self.y)], self.got_y, 3, self.chips["y"][0])]

    def z_copies(self):
        return [
            self.copy(self.got_x.at[self.piece(p, self.y)], self.got_z.at[n], 4 + n, at)
            for n, (p, at) in enumerate(zip(self.chips["pieces"], self.chips["z"]))
        ]

    def extra_copies(self):
        src = self.got_x.at[self.piece(self.z, self.y)]
        return [
            self.copy(src, self.got_e.at[n], n, at, True) for n, at in enumerate(self.chips["e"])
        ]

    def back_z_copies(self):
        part = self.out.at[self.piece(self.z, self.y), self.lanes]
        return [self.copy(part, part, 7 + n, at) for n, at in enumerate(self.chips["z"])]

    def back_y_copies(self):
        part = self.out.at[self.half(self.y), self.lanes]
        return [self.copy(part, part, 10, self.chips["y"][0])]

    def core(self):
        for cp in self.core_copies():
            cp.start()

    def across_x(self):
        for cp in self.core_copies():
            cp.wait_recv()
        far = 1 - self.x
        block = 2 * far + self.c
        self.grad[block] = (
            self.grad[block].astype(float_type) + self.got_core[far].astype(float_type)
        ).astype(low_type)
        self.x_copies()[0].start()

    def chip_sum(self, rows):
        return (
            self.grad[2 * self.x + self.c, rows].astype(float_type)
            + self.got_core[self.x, rows].astype(float_type)
            + self.got_x[rows].astype(float_type)
        )

    def across_y(self):
        self.x_copies()[0].wait_recv()
        rows = self.half(1 - self.y)
        self.got_x[rows] = self.chip_sum(rows).astype(low_type)
        self.y_copies()[0].start()
        self.own[...] = self.chip_sum(self.half(self.y))

    def across_z(self):
        self.y_copies()[0].wait_recv()
        v = self.own[...] + self.got_y[...].astype(float_type)
        self.own[...] = v
        self.got_x[self.half(self.y)] = v.astype(low_type)
        for cp in self.z_copies():
            cp.start()

    def back_z(self):
        for cp in self.z_copies():
            cp.wait_recv()
        v = self.own[self.piece(self.z)]
        for n in range(3):
            v = v + self.got_z[n].astype(float_type)
        if self.chips["e"]:
            self.got_x[self.piece(self.z, self.y)] = v.astype(low_type)
            for cp in self.extra_copies():
                cp.start()
            for n, cp in enumerate(self.extra_copies()):
                cp.wait_recv()
                v = v + self.got_e[n].astype(float_type)
        self.out[self.piece(self.z, self.y), self.lanes] = v.astype(low_type)
        for cp in self.back_z_copies():
            cp.start()

    def back_y(self):
        for cp in self.back_z_copies():
            cp.wait_recv()
        self.back_y_copies()[0].start()

    def end(self):
        self.back_y_copies()[0].wait_recv()

    def drain(self):
        for cp in (
            self.core_copies() + self.x_copies() + self.y_copies() + self.z_copies()
            + self.extra_copies() + self.back_z_copies() + self.back_y_copies()
        ):
            cp.wait_send()


def block_kernel(
    x_ref, cot_ref, *rest,
):
    lines, rest = rest[:11], rest[11:]
    count_ref, index_ref, label_ref = rest[:3]
    (w1_any, w2_any, jw_any, ow_any, ew_any, ct_any,
    res_ref, gx_ref, gw1_ref, gw2_ref, go_ref, gv_ref, ge_ref, gc_ref, geo_ref,
    w1, w2, jw, ow, ew, ct, ones, hid, mid, mod, emb, act1_t, act2_t, st, m1, m3, got,
    att, att_t, kv, kv_t, q8, d_out_t, qm, dom, s_ref, eb, dsb, mix_t, dq_t, dq, dkv,
    got_core, got_x, ag, q_sum, kv_sum, o_sum, gjo,
    grad, slope_grad, gs, mg,
    gw, w_core, w_got_x, w_own, w_got_y, w_got_z, w_got_e,
    o_core, o_got_x, o_own, o_got_y, o_got_z, o_got_e,
    v_own, v_row, v_one, v_y, v_two, v_z, v_three, v_e, g_row, gat, left, hot,
    vec_ref, prep_ref, wsem, ssem, rsem, gsend, grecv, asem, bsem, cs, cr, es, er, vs, vr, gsem,
    hsem) = rest[3:]
    images, pixels, channels = x_ref.shape
    width = 32
    edge = pixels - width
    rows_in = pixels // width
    whole = 4 * pixels
    entries = float(whole * (channels // GROUPS))
    half = math.sqrt(0.5)
    quarter = 9 * channels // 4
    padded = gw.shape[2]
    chunk = 128
    pair_lanes = 2 * HEAD
    pairs = channels // pair_lanes
    i, r, c, who = peers()
    chips = chip_peers(i, r)
    place = (c, lax.div(r, 2), chips)
    inner = pl.multiple_of(edge * (1 - c), width)
    outer = pl.multiple_of(edge * c, width)
    inner_halo = pl.multiple_of((pixels + width) * (1 - c), width)
    outer_halo = pl.multiple_of((pixels + width) * c, width)
    outer_live = jnp.logical_and(r > 0, r < 3)
    loads = {
        name: pltpu.make_async_copy(src, dst, wsem.at[n])
        for n, (name, src, dst) in enumerate((
            ("ct", ct_any, ct), ("ew", ew_any, ew), ("w1", w1_any, w1), ("w2", w2_any, w2),
            ("jw", jw_any, jw), ("ow", ow_any, ow),
        ))
    }
    for cp in loads.values():
        cp.start()
    barrier = pltpu.get_barrier_semaphore()
    greeted = list(who.values()) + chips["y"] + chips["z"] + chips["e"]
    for at in greeted:
        pl.semaphore_signal(barrier, inc=1, device_id=at, device_id_type=MESH)

    abuf = grad.at[0]

    def dot(a, b):
        return jnp.dot(a, b, preferred_element_type=float_type)

    def dot_nt(a, b):
        return lax.dot_general(a, b, contract_cols, preferred_element_type=float_type)

    def vec(n):
        return vec_ref[n : n + 1, :]

    def col_sum(v):
        return jnp.sum(v, axis=0, keepdims=True)

    def slope_of(pre):
        s = 0.5 * jnp.tanh(0.5 * pre) + 0.5
        return s * (1.0 + pre * (1.0 - s))

    def remote(src, dst, send, recv, at):
        return pltpu.make_async_remote_copy(
            src, dst, send, recv, device_id=at, device_id_type=MESH
        )

    def start(copies):
        for cp in copies:
            cp.start()

    def arrived(copies):
        for cp in copies:
            cp.wait_recv()

    def some_images(step, first, last):
        def run(b, _):
            step(b)
            return 0

        lax.fori_loop(first, last, run, 0)

    def each_image(step):
        some_images(step, 0, images)

    message_rows = (48, 48, 48, 48, 48, 16, 48)

    def copies(p, b):
        full, stat = pl.ds(0, message_rows[p]), pl.ds(0, 16)
        return [
            remote(
                src.at[p, b, rows], got.at[p, b, k - 1, rows], ssem.at[p, b, k - 1],
                rsem.at[p, b, k - 1], who[k],
            )
            for k, src, rs in ((1, m1, full), (2, m1, stat), (3, m3, full))
            for rows in (rs,)
        ]

    def fill_message(p, b, first, second, edges=None):
        packed = pack_stats(first, second)
        m1[p, b, 0:16] = packed
        m3[p, b, 0:16] = packed
        if edges is not None:
            m1[p, b, 16:48] = edges(inner).astype(low_type)
            m3[p, b, 16:48] = edges(outer).astype(low_type)

    def send(p, b, first, second, edges=None):
        fill_message(p, b, first, second, edges)
        start(copies(p, b))

    def receive(p, b):
        arrived(copies(p, b))
        parts = [m1[p, b, 0:16]] + [got[p, b, k, 0:16] for k in range(3)]
        return combine_stats(parts, ones[...], entries)

    def receive_scale(p, b):
        first, second = receive(p, b)
        scaled = lax.rsqrt(second - first * first + norm_eps)
        st[b, 2 * p : 2 * p + 1] = first
        st[b, 2 * p + 1 : 2 * p + 2] = scaled
        return first, scaled

    def far_rows(p, b, k):
        return got[p, b, k, 16:48].astype(float_type)

    def fill_halo(buf, value):
        fill_row(buf, inner_halo, value(0), channels, width)
        fill_row(buf, outer_halo, jnp.where(outer_live, value(2), 0.0), channels, width)

    def convolve(w):
        depth = 3 * channels
        return sum(
            dot(abuf[width * dy : width * dy + pixels, :], w[depth * dy : depth * (dy + 1), :])
            for dy in range(3)
        )

    def data_grad(buf, b, w):
        total = None
        for dy in range(3):
            for dx in range(3):
                tap = 3 * dy + dx
                more = dot_nt(
                    buf[b, (2 - dy) * width : (2 - dy) * width + pixels,
                        (2 - dx) * channels : (3 - dx) * channels],
                    w[tap * channels : (tap + 1) * channels, :],
                )
                total = more if total is None else total + more
        return total

    def kernel_grad(act_t, buf, base):
        for dy in range(3):
            for dx in range(3):
                tap = 3 * dy + dx
                at = (2 - dx) * channels
                g = None
                for b in range(images):
                    more = dot(
                        act_t[:, b * pixels : (b + 1) * pixels],
                        buf[b, (2 - dy) * width : (2 - dy) * width + pixels, at : at + channels],
                    )
                    g = more if g is None else g + more
                g = g.astype(low_type)
                for m in range(4):
                    lo = max(tap * channels, m * quarter)
                    hi = min((tap + 1) * channels, (m + 1) * quarter)
                    for n in range(3 if lo < hi else 0):
                        gw[base + n, m, lo - m * quarter : hi - m * quarter] = g[
                            lo - tap * channels : hi - tap * channels, 128 * n : 128 * n + 128
                        ]

    def reduction(out, lanes, n, q, refs):
        return Reduction(out, lanes, n, q, refs, who, place, cs, cr, es, er)

    refs = (gw, w_core, w_got_x, w_own, w_got_y, w_got_z, w_got_e)
    red2 = [reduction(gw2_ref, slice(128 * n, 128 * n + 128), n, n, refs) for n in range(3)]
    red1 = [reduction(gw1_ref, slice(128 * n, 128 * n + 128), n + 3, n + 3, refs) for n in range(3)]
    refs = (gjo, o_core, o_got_x, o_own, o_got_y, o_got_z, o_got_e)
    red0 = reduction(go_ref, slice(0, channels), None, 6, refs)
    zs, extras = chips["z"], chips["e"]

    def small_row_copies(s):
        return [
            remote(v_own.at[s], v_row.at[s, k - 1], vs.at[s, k - 1], vr.at[s, k - 1], who[k])
            for k in (1, 2, 3)
        ]

    def small_y_copies(s):
        return [remote(v_one.at[s], v_y.at[s], vs.at[s, 3], vr.at[s, 3], chips["y"][0])]

    def small_z_copies(s):
        return [
            remote(v_two.at[s], v_z.at[s, n], vs.at[s, 4 + n], vr.at[s, 4 + n], at)
            for n, at in enumerate(zs)
        ]

    def small_e_copies(s):
        return [
            remote(v_three.at[s], v_e.at[s, n], vs.at[s, 7 + n], vr.at[s, 7 + n], at)
            for n, at in enumerate(extras)
        ]

    def small_row(s):
        v_own[s] = gs[...]
        start(small_row_copies(s))

    def small_y(s):
        arrived(small_row_copies(s))
        v_one[s] = v_own[s] + v_row[s, 0] + v_row[s, 1] + v_row[s, 2]
        start(small_y_copies(s))

    def small_z(s):
        arrived(small_y_copies(s))
        v_two[s] = v_one[s] + v_y[s]
        start(small_z_copies(s))

    def small_end(s):
        arrived(small_z_copies(s))
        v_three[s] = v_two[s] + v_z[s, 0] + v_z[s, 1] + v_z[s, 2]
        total = v_three[s]
        if extras:
            start(small_e_copies(s))
            arrived(small_e_copies(s))
            for n in range(len(extras)):
                total = total + v_e[s, n]
        gv_ref[s] = total

    def gather_row_copies():
        return [
            remote(mg, g_row.at[k - 1], gsem.at[k - 1], hsem.at[k - 1], who[k])
            for k in (1, 2, 3)
        ]

    def gather_copies():
        blocks = [pl.ds(i, 1), pl.ds(pl.multiple_of(i - lax.rem(i, 2), 2), 2)]
        blocks.append(pl.ds(pl.multiple_of(i - lax.rem(i, 8), 8), 8))
        found = []
        for rows, places in zip(blocks, (chips["y"], zs, extras)):
            for at in places:
                n = 3 + len(found)
                found.append(remote(gat.at[rows], gat.at[rows], gsem.at[n], hsem.at[n], at))
        return found

    def gather_row():
        start(gather_row_copies())

    def gather_y():
        arrived(gather_row_copies())
        gat[i] = emb[...] + mg[...] + g_row[0] + g_row[1] + g_row[2]
        start(gather_copies()[:1])

    def gather_z():
        arrived(gather_copies()[:1])
        start(gather_copies()[1:4])

    def gather_end():
        arrived(gather_copies()[1:4])
        start(gather_copies()[4:])
        arrived(gather_copies()[4:])

    def three_terms(v):
        a = v.astype(low_type)
        b = (v - a.astype(float_type)).astype(low_type)
        d = (v - a.astype(float_type) - b.astype(float_type)).astype(low_type)
        return jnp.concatenate([a, b, d], axis=0)

    def embedding():
        ge_ref[...] = jnp.zeros(ge_ref.shape, float_type)
        gc_ref[...] = jnp.zeros(gc_ref.shape, float_type)
        geo_ref[...] = jnp.zeros(geo_ref.shape, float_type)
        lax.fori_loop(0, gat.shape[0] // 8, embedding_part, 0)

    def embedding_part(part_of, _):
        every = 64
        full = gat[pl.ds(pl.multiple_of(part_of * 8, 8), 8)].reshape(every, 2 * channels)
        place_of = lax.rem(lax.broadcasted_iota(jnp.int32, (every, 2 * channels), 0), 8)
        live = place_of < images
        grad = jnp.where(live, full, 0.0)
        held = jnp.where(live, pltpu.roll(full, every - images, 0), 0.0)
        act = jnp.where(live, half_silu(held), 0.0).astype(low_type)
        left[...] = jnp.concatenate([act, act, act], axis=0).T
        terms = three_terms(grad)
        size = 2 * channels // 4
        own = pl.ds(pl.multiple_of(r * size, size), size)
        ge_ref[...] += jnp.dot(left[own, :], terms, preferred_element_type=float_type)
        geo_ref[...] += jnp.broadcast_to(jnp.sum(grad, axis=0, keepdims=True), geo_ref.shape)
        active = lax.dot_general(terms, ew[...], contract_cols, preferred_element_type=float_type)
        active = active[0:every] + active[every : 2 * every] + active[2 * every :]
        back = jnp.where(live, active * slope_of(held), 0.0)
        classes = gc_ref.shape[0]
        row_of = lax.rem(lax.broadcasted_iota(jnp.int32, (every, 128), 0), 8)
        label = jnp.full((every, 128), -1.0, float_type)
        for b in range(images):
            rolled = pltpu.roll(full[:, 256 * b : 256 * b + 128], every - 2 * images + b, 0)
            label = jnp.where(row_of == b, rolled, label)
        for n in range(hot.shape[0] // 128):
            kind = lax.broadcasted_iota(jnp.int32, (every, 128), 1) + 128 * n + r * classes
            hit = jnp.where(label == kind.astype(float_type), 1.0, 0.0).astype(low_type)
            hot[128 * n : 128 * (n + 1), :] = jnp.concatenate([hit, hit, hit], axis=0).T
        found = jnp.dot(hot[...], three_terms(back), preferred_element_type=float_type)
        gc_ref[...] += found[0:classes]
        return 0

    def embed_forward():
        row = lax.broadcasted_iota(jnp.int32, (8, 2 * channels), 0)
        lane_of = lax.broadcasted_iota(jnp.int32, (8, channels), 1).astype(float_type)

        def spread(ref, other):
            v = jnp.full((8, channels), other, float_type)
            for b in range(images):
                v = jnp.where(row[:, :channels] == b, ref[b].astype(float_type), v)
            return v

        position = (spread(index_ref, 0.0) + 1.0) / (spread(count_ref, 2.0) - 1.0)
        low_root = sigma_least ** (1.0 / sigma_power)
        high_root = sigma_most ** (1.0 / sigma_power)
        root = low_root + position * (high_root - low_root)
        square = root * root
        noise_time = 250.0 * jnp.log(square * square * square * root)
        angles = noise_time * jnp.exp(lane_of * (-math.log(10000.0) / channels))
        features = jnp.concatenate([jnp.cos(angles), jnp.sin(angles)], axis=1)
        count = ct.shape[0]
        label = spread(label_ref, -1.0)[:, 0:1]
        kinds = lax.broadcasted_iota(jnp.int32, (8, count), 1).astype(float_type)
        one_hot = jnp.where(label == kinds, 1.0, 0.0).astype(low_type)
        loads["ct"].wait()
        embedded = features + dot(one_hot, ct[...])
        live = row < images
        embed_act = half_silu(embedded).astype(low_type)
        loads["ew"].wait()
        offset = jnp.concatenate([vec(11), vec(12)], axis=1)
        mod[...] = dot(embed_act, ew[...]) + offset
        rows = pltpu.roll(jnp.where(live, embedded, 0.0), images, 0)
        part_of = lax.broadcasted_iota(jnp.int32, (8, 2 * channels), 1)
        marks = jnp.zeros((8, 2 * channels), float_type)
        for b in range(images):
            here = jnp.logical_and(row == 2 * images, part_of >= 256 * b)
            marks = jnp.where(here, label_ref[b].astype(float_type), marks)
        emb[...] = rows + marks

    at = 0
    for line in lines:
        v = line[...].astype(float_type).reshape(1, line.shape[0])
        for n in range(line.shape[0] // channels):
            vec_ref[at : at + 1] = v[:, n * channels : (n + 1) * channels]
            at += 1
    ones[...] = block_ones(channels, channels // GROUPS)
    gs[...] = jnp.zeros(gs.shape, float_type)
    mg[...] = jnp.zeros(mg.shape, float_type)

    def clear(n, _):
        for m in range(4):
            gw[n, m, quarter:padded] = jnp.zeros((padded - quarter, 128), low_type)
        return 0

    lax.fori_loop(0, 6, clear, 0)

    @each_image
    def _(b):
        v = x_ref[b].astype(float_type)
        fill_message(0, b, col_sum(v), col_sum(v * v), lambda at: x_ref[b, pl.ds(at, width)])
        none = jnp.zeros((1, channels), float_type)
        fill_message(6, b, none, none, lambda at: cot_ref[b, pl.ds(at, width)])

    embed_forward()
    pl.semaphore_wait(barrier, len(greeted))

    @each_image
    def _(b):
        start(copies(0, b))

    @each_image
    def _(b):
        start(copies(6, b))

    loads["ow"].wait()

    @each_image
    def _(b):
        d_out_t[b] = dot_nt(cot_ref[b], ow[...]).T.astype(low_type)

    loads["w1"].wait()

    @each_image
    def _(b):
        centre, scaled = receive_scale(0, b)
        slope = scaled * vec(0)
        shift = vec(1)

        def activate(v):
            return half_silu((v - centre) * slope + shift)

        for row in range(rows_in):
            v = activate(x_ref[b, row * width : (row + 1) * width].astype(float_type))
            fill_row(abuf, (row + 1) * width, v, channels, width)
        fill_halo(abuf, lambda k: activate(far_rows(0, b, k)))
        hidden = convolve(w1) + vec(2)
        hid[b] = hidden
        send(
            1, b, col_sum(hidden), col_sum(hidden * hidden),
            lambda at: hid[b, pl.ds(at, width)],
        )
        own = pl.ds(pl.multiple_of(b * pixels, pixels), pixels)
        act1_t[:, own] = abuf[width : width + pixels, channels : 2 * channels].T

    def block(n):
        return pl.ds(pl.multiple_of(n * pixels, pixels), pixels)

    mate = r + 1 - 2 * c
    across = lax.rem(r + 2, 4)

    def gather(b, n, rows):
        return remote(
            att.at[b, rows], att.at[b, rows], gsend.at[b, n], grecv.at[b, n], who[(1, 2, 1)[n]]
        )

    def shares(b):
        return [gather(b, n, block(rows)) for n, rows in enumerate((r, r, across))]

    def arrivals(b):
        rows = (mate, across, lax.rem(mate + 2, 4))
        return [gather(b, n, block(w)) for n, w in enumerate(rows)]

    def share(b):
        centre, scaled = receive_scale(2, b)
        slope = scaled * vec(6)
        att[b, block(r)] = ((mid[b] - centre) * slope + vec(7)).astype(low_type)
        start(shares(b)[:2])

    loads["w2"].wait()
    loads["jw"].wait()

    @each_image
    def _(b):
        @pl.when(b == images - 1)
        def _():
            share(0)

        centre, scaled = receive_scale(1, b)
        grow = 1.0 + mod[pl.ds(b, 1), 0:channels]
        slope = scaled * vec(3) * grow
        shift = vec(4) * grow + mod[pl.ds(b, 1), channels:]

        def activate(v):
            return half_silu((v - centre) * slope + shift)

        for row in range(rows_in):
            v = activate(hid[b, row * width : (row + 1) * width])
            fill_row(abuf, (row + 1) * width, v, channels, width)
        fill_halo(abuf, lambda k: activate(far_rows(1, b, k)))
        middle = (convolve(w2) + vec(5) + x_ref[b].astype(float_type)) * half
        mid[b] = middle
        send(
            2, b, col_sum(middle), col_sum(middle * middle),
            lambda at: mid[b, pl.ds(at, width)],
        )
        own = pl.ds(pl.multiple_of(b * pixels, pixels), pixels)
        act2_t[:, own] = abuf[width : width + pixels, channels : 2 * channels].T

    part = att

    def forward(b):
        arrivals(b)[1].wait_recv()
        shares(b)[2].start()

    def sums_core(b):
        return [
            remote(
                part.at[b, block(2 * n + 1 - c)], got_core.at[b, n], asem.at[b, n],
                bsem.at[b, n], who[1],
            )
            for n in range(2)
        ]

    def sum_x(b):
        far = block(2 * (1 - lax.div(r, 2)) + c)
        return remote(part.at[b, far], got_x.at[b], asem.at[b, 2], bsem.at[b, 2], who[2])

    def pass_on(b):
        x = lax.div(r, 2)
        arrived(sums_core(b))
        far = 1 - x
        rows = block(2 * far + c)
        part[b, rows] = (
            part[b, rows].astype(float_type) + got_core[b, far].astype(float_type)
        ).astype(low_type)
        sum_x(b).start()
        ag[b] = part[b, block(r)].astype(float_type) + got_core[b, x].astype(float_type)

    def queries(b):
        q = (dot(att[b, block(r)], jw[:, :channels]) + vec(8)).astype(low_type)
        q8[b] = (q.astype(float_type) * HEAD ** (-0.5)).astype(low_type)

    some_images(share, 1, images)
    each_image(queries)
    lane = lax.broadcasted_iota(jnp.int32, (pixels, pair_lanes), 1)

    def masked(v):
        return jnp.concatenate(
            [jnp.where(lane < HEAD, v, 0.0), jnp.where(lane >= HEAD, v, 0.0)], axis=0
        ).astype(low_type)

    q_sum[...] = jnp.zeros(q_sum.shape, float_type)
    kv_sum[...] = jnp.zeros(kv_sum.shape, float_type)
    o_sum[...] = jnp.zeros(o_sum.shape, float_type)
    att_t[channels:] = jnp.ones((16, whole), low_type)
    forward(0)

    @each_image
    def _(b):
        a = arrivals(b)
        a[0].wait_recv()
        a[2].wait_recv()
        bias = jnp.concatenate([jnp.zeros((1, channels), float_type), vec(9)], axis=1)
        for n in range(4):
            rows = pl.ds(n * pixels, pixels)
            kv[rows] = (dot(att[b, rows], jw[:, channels:]) + bias).astype(low_type)
        for n in range(2 * channels // 128):
            cols = pl.ds(n * 128, 128)
            kv_t[cols, :] = kv[:, cols].T

        @pl.when(b > 0)
        def _():
            pass_on(b - 1)

        def one_pair(t, _):
            lanes = pl.ds(pl.multiple_of(t * pair_lanes, pair_lanes), pair_lanes)
            v_lanes = pl.ds(pl.multiple_of(channels + t * pair_lanes, pair_lanes), pair_lanes)
            qm[...] = masked(q8[b, :, lanes].astype(float_type))
            peak = None
            for n in range(whole // chunk):
                rows = pl.ds(n * chunk, chunk)
                s = dot_nt(kv[rows, lanes], qm[...])
                s_ref[rows] = s
                top = jnp.max(s.reshape(chunk // 8, 8, 2 * pixels), axis=0)
                peak = top if peak is None else jnp.maximum(peak, top)
            peak = jnp.max(peak, axis=0, keepdims=True)
            total = None
            for n in range(whole // chunk):
                rows = pl.ds(n * chunk, chunk)
                e = jnp.exp(s_ref[rows] - peak)
                eb[rows] = e.astype(low_type)
                more = jnp.sum(e.reshape(chunk // 8, 8, 2 * pixels), axis=0)
                total = more if total is None else total + more
            over = 1.0 / jnp.sum(total, axis=0, keepdims=True)
            inner_of, scaled = [], []
            for j in range(2):
                head = pl.ds(pl.multiple_of(t * pair_lanes + j * HEAD, HEAD), HEAD)
                v_head = pl.ds(pl.multiple_of(channels + t * pair_lanes + j * HEAD, HEAD), HEAD)
                cols = slice(j * pixels, (j + 1) * pixels)
                mt = dot(kv_t[v_head, :], eb[:, cols]) * over[:, cols]
                mix_t[head] = mt.astype(low_type)
                g = (d_out_t[b, head].astype(float_type) * over[:, cols]).astype(low_type).astype(float_type)
                inner_of.append(col_sum(g * mt))
                scaled.append(g)
            inner_of = jnp.concatenate(inner_of, axis=1)
            dom[...] = masked(jnp.concatenate(scaled, axis=0).T)
            for n in range(whole // chunk):
                rows = pl.ds(n * chunk, chunk)
                dp = dot_nt(kv[rows, v_lanes], dom[...])
                dsb[rows] = (eb[rows].astype(float_type) * (dp - inner_of)).astype(low_type)
            for j in range(2):
                head = pl.ds(pl.multiple_of(t * pair_lanes + j * HEAD, HEAD), HEAD)
                cols = slice(j * pixels, (j + 1) * pixels)
                dq_t[head] = dot(kv_t[head, :], dsb[:, cols]) * HEAD ** (-0.5)
            dkv[:, lanes] = dot(dsb[...], qm[...]).astype(low_type)
            dkv[:, v_lanes] = dot(eb[...], dom[...]).astype(low_type)
            return 0

        lax.fori_loop(0, pairs, one_pair, 0)

        @pl.when(b + 1 < images)
        def _():
            forward(b + 1)

        dq[...] = dq_t[...].T.astype(low_type)
        att_t[0:channels] = att[b].T
        for cp in shares(b):
            cp.wait_send()
        for n in range(4):
            rows = pl.ds(n * pixels, pixels)
            part[b, rows] = dot_nt(dkv[rows], jw[:, channels:]).astype(low_type)
        part[b, block(r)] = (
            part[b, block(r)].astype(float_type) + dot_nt(dq[...], jw[:, :channels])
        ).astype(low_type)
        start(sums_core(b))
        q_sum[...] += dot(att_t[:, block(r)], dq[...])
        kv_sum[...] += dot(att_t[...], dkv[...])
        o_sum[...] += dot(mix_t[...], cot_ref[b])
        mixed = mix_t[...].T
        res_ref[b] = (mid[b] + dot(mixed, ow[...]) + vec(10)).astype(low_type)

    def pack_weights():
        part_rows = channels // 4
        every = (q_sum[0:channels], kv_sum[0:channels, :channels], kv_sum[0:channels, channels:], o_sum[...])
        for n, v in enumerate(every):
            for m in range(4):
                gjo[m, n * part_rows : (n + 1) * part_rows] = v[
                    m * part_rows : (m + 1) * part_rows
                ].astype(low_type)
        gs[8:9] = q_sum[channels : channels + 1]
        gs[9:10] = kv_sum[channels : channels + 1, channels:]
        gs[10:11] = col_sum(jnp.sum(cot_ref[...].astype(float_type), axis=0))

    def attend_sums(b):
        sum_x(b).wait_recv()
        u = ag[b] + got_x[b].astype(float_type)
        ag[b] = u
        first = col_sum(u)
        second = col_sum(u * ((mid[b] - st[b, 4:5]) * st[b, 5:6]))
        gs[6:7] += second
        gs[7:8] += first
        send(3, b, first * vec(6), second * vec(6), lambda at: ag[b, pl.ds(at, width)])

    def branch_grad(b):
        first, second = receive(3, b)
        arrived(copies(6, b))
        centre, scaled = st[b, 4:5], st[b, 5:6]

        def grad_of(cot, u, v):
            return (cot + scaled * (u * vec(6) - first - (v - centre) * scaled * second)) * half

        total = jnp.zeros((1, channels), float_type)
        for row in range(rows_in):
            rows = pl.ds(row * width, width)
            v = grad_of(cot_ref[b, rows].astype(float_type), ag[b, rows], mid[b, rows])
            ag[b, rows] = v
            v = v.astype(low_type).astype(float_type)
            fill_row(grad.at[b], (row + 1) * width, v, channels, width)
            total += col_sum(v)
        gs[5:6] += total
        fill_halo(
            grad.at[b],
            lambda k: grad_of(far_rows(6, b, k), far_rows(3, b, k), far_rows(2, b, k)),
        )

    def branch_back(b):
        upstream = data_grad(grad, b, w2)
        grow = 1.0 + mod[pl.ds(b, 1), 0:channels]
        normed = (hid[b] - st[b, 2:3]) * st[b, 3:4]
        pre = (normed * vec(3) + vec(4)) * grow + mod[pl.ds(b, 1), channels:]
        v = upstream * slope_of(pre)
        slope_grad[b] = v
        first, second = col_sum(v), col_sum(v * normed)
        mg[pl.ds(b, 1), 0:channels] = vec(3) * second + vec(4) * first
        mg[pl.ds(b, 1), channels:] = first
        first, second = grow * first, grow * second
        gs[3:4] += second
        gs[4:5] += first
        send(
            4, b, first * vec(3), second * vec(3),
            lambda at: slope_grad[b, pl.ds(at, width)],
        )

    def hidden_grad(b):
        first, second = receive(4, b)
        centre, scaled = st[b, 2:3], st[b, 3:4]
        gain = (1.0 + mod[pl.ds(b, 1), 0:channels]) * vec(3)

        def grad_of(u, v):
            return scaled * (u * gain - first - (v - centre) * scaled * second)

        total = jnp.zeros((1, channels), float_type)
        for row in range(rows_in):
            rows = pl.ds(row * width, width)
            v = grad_of(slope_grad[b, rows], hid[b, rows]).astype(low_type).astype(float_type)
            fill_row(grad.at[b], (row + 1) * width, v, channels, width)
            total += col_sum(v)
        gs[2:3] += total
        fill_halo(grad.at[b], lambda k: grad_of(far_rows(4, b, k), far_rows(1, b, k)))

    def hidden_back(b):
        upstream = data_grad(grad, b, w1)
        normed = (x_ref[b].astype(float_type) - st[b, 0:1]) * st[b, 1:2]
        v = upstream * slope_of(normed * vec(0) + vec(1))
        slope_grad[b] = v
        first, second = col_sum(v), col_sum(v * normed)
        gs[0:1] += second
        gs[1:2] += first
        send(5, b, first * vec(0), second * vec(0))

    def images_grad(b):
        first, second = receive(5, b)
        scaled = st[b, 1:2]
        normed = (x_ref[b].astype(float_type) - st[b, 0:1]) * scaled
        gx_ref[b] = ag[b] + scaled * (slope_grad[b] * vec(0) - first - normed * second)

    pass_on(images - 1)
    some_images(attend_sums, 0, images - 1)
    pack_weights()
    red0.core()
    some_images(attend_sums, images - 1, images)
    red0.across_x()
    some_images(branch_grad, 0, images - 1)
    some_images(branch_back, 0, images - 1)
    some_images(branch_grad, images - 1, images)
    kernel_grad(act2_t, grad, 0)
    red2[1].core()
    some_images(branch_back, images - 1, images)
    small_row(0)
    gather_row()
    red0.across_y()
    some_images(hidden_grad, 0, images - 1)
    red2[1].across_x()
    red2[0].core()
    red2[2].core()
    some_images(hidden_grad, images - 1, images)
    red2[0].across_x()
    kernel_grad(act1_t, grad, 3)
    red0.across_z()
    small_y(0)
    gather_y()
    red1[1].core()
    red2[2].across_x()
    red1[0].core()
    red1[2].core()
    some_images(hidden_back, 0, images - 1)
    red1[0].across_x()
    red1[1].across_x()
    red2[1].across_y()
    some_images(hidden_back, images - 1, images)
    red1[2].across_x()
    small_z(0)
    gather_z()
    small_row(1)
    red0.back_z()
    red2[0].across_y()
    red2[1].across_z()
    small_end(0)
    gather_end()
    embedding()
    red2[2].across_y()
    red0.back_y()
    red2[0].across_z()
    red2[1].back_z()
    red2[2].across_z()
    red1[0].across_y()
    red2[0].back_z()
    red2[1].back_y()
    red0.end()
    red1[1].across_y()
    red2[2].back_z()
    each_image(images_grad)
    red1[0].across_z()
    red2[0].back_y()
    red2[1].end()
    red1[2].across_y()
    red1[1].across_z()
    red2[2].back_y()
    small_y(1)
    red2[0].end()
    red1[0].back_z()
    red1[2].across_z()
    red1[1].back_z()
    red2[2].end()
    red1[0].back_y()
    small_z(1)
    red1[2].back_z()
    red1[1].back_y()
    red1[0].end()
    small_end(1)
    red1[2].back_y()
    red1[1].end()
    red1[2].end()

    @each_image
    def _(b):
        sent = sums_core(b) + [sum_x(b)]
        for p in range(7):
            sent += copies(p, b)
        for cp in sent:
            cp.wait_send()

    for red in [red0] + red1 + red2:
        red.drain()
    for s in range(2):
        for cp in small_row_copies(s) + small_y_copies(s) + small_z_copies(s) + small_e_copies(s):
            cp.wait_send()
    for cp in gather_row_copies() + gather_copies():
        cp.wait_send()


def block_call(x, cot, lines, scalars, w1, w2, jw, ow, ew, ct):
    images, pixels, channels = x.shape
    span = pixels + 64
    whole = 4 * pixels
    padded = -(-9 * channels // 4 // 128) * 128
    every = lax.axis_size("img")
    more = every // 8
    some = max(more - 1, 1)
    classes = ct.shape[0]
    vm = pl.BlockSpec(memory_space=pltpu.VMEM)
    hbm = pl.BlockSpec(memory_space=pl.ANY)

    def low(*shape):
        return pltpu.VMEM(shape, low_type)

    def wide(*shape):
        return pltpu.VMEM(shape, float_type)

    def dma(*shape):
        return pltpu.SemaphoreType.DMA(shape)

    def out(*shape, kind=float_type):
        return jax.ShapeDtypeStruct(shape, kind)

    return pl.pallas_call(
        block_kernel,
        out_shape=(
            out(*x.shape, kind=low_type), out(*x.shape), out(padded, channels, kind=low_type),
            out(padded, channels, kind=low_type), out(channels, channels, kind=low_type),
            out(2, 16, channels), out(2 * channels // 4, 2 * channels),
            out(classes // 4, 2 * channels), out(8, 2 * channels),
        ),
        in_specs=[vm] * (2 + len(lines)) + [pl.BlockSpec(memory_space=pltpu.SMEM)] * 3 + [hbm] * 6,
        out_specs=(vm,) * 9,
        scratch_shapes=[
            low(*w1.shape), low(*w2.shape), low(*jw.shape), low(*ow.shape), low(*ew.shape),
            low(*ct.shape), low(channels, channels), wide(*x.shape), wide(*x.shape),
            wide(8, 2 * channels), wide(8, 2 * channels),
            low(channels, images * pixels), low(channels, images * pixels),
            wide(images, 8, channels), low(7, images, 48, channels), low(7, images, 48, channels),
            low(7, images, 3, 48, channels),
            low(images, whole, channels), low(channels + 16, whole), low(whole, 2 * channels),
            low(2 * channels, whole), low(*x.shape), low(images, channels, pixels),
            low(2 * pixels, 2 * HEAD), low(2 * pixels, 2 * HEAD), wide(whole, 2 * pixels),
            low(whole, 2 * pixels), low(whole, 2 * pixels), low(channels, pixels),
            wide(channels, pixels), low(pixels, channels), low(whole, 2 * channels),
            low(images, 2, pixels, channels), low(*x.shape), wide(*x.shape),
            wide(channels + 16, channels),
            wide(channels + 16, 2 * channels), wide(channels, channels), low(4, channels, channels),
            low(images, span, 3 * channels), wide(*x.shape), wide(16, channels), wide(8, 2 * channels),
            low(6, 4, padded, 128), low(6, 2, padded, 128), low(6, padded, 128),
            wide(6, padded // 2, 128), low(6, padded // 2, 128), low(6, 3, padded // 8, 128),
            low(6, some, padded // 8, 128),
            low(2, channels, channels), low(channels, channels), wide(channels // 2, channels),
            low(channels // 2, channels), low(3, channels // 8, channels),
            low(some, channels // 8, channels),
            wide(2, 16, channels), wide(2, 3, 16, channels), wide(2, 16, channels),
            wide(2, 16, channels), wide(2, 16, channels), wide(2, 3, 16, channels),
            wide(2, 16, channels), wide(2, some, 16, channels), wide(3, 8, 2 * channels),
            wide(every, 8, 2 * channels), low(2 * channels, 192), low(256, 192), wide(16, channels), wide(8, 2 * channels),
            dma(6), dma(7, images, 3), dma(7, images, 3), dma(images, 3), dma(images, 3),
            dma(images, 3), dma(images, 3), dma(7, 11), dma(7, 11), dma(7, some), dma(7, some),
            dma(2, 6 + more), dma(2, 6 + more), dma(6 + more), dma(6 + more),
        ],
        compiler_params=pltpu.CompilerParams(
            collective_id=0, has_side_effects=True, vmem_limit_bytes=62 << 20
        ),
        name="block",
    )(x, cot, *lines, *scalars, w1, w2, jw, ow, ew, ct)


def finish_kernel(
    res, gx, gw1, gw2, go, gv, ge, gc, geo,
    res_out, gx_out, first_gain, first_shift, first_kernel, first_offset, embed_weight,
    embed_offset, class_table, second_gain, second_shift, second_kernel, second_offset,
    third_gain, third_shift, joint_weight, joint_offset, output_weight, output_offset, sems,
):
    r = lax.axis_index("row")
    moves = [
        pltpu.make_async_copy(src, dst, sems.at[n])
        for n, (src, dst) in enumerate(
            ((res, res_out), (gx, gx_out), (ge, embed_weight), (gc, class_table))
        )
    ]
    for cp in moves:
        cp.start()
    first_kernel[...] = gw1[0 : first_kernel.shape[0]].astype(float_type)
    second_kernel[...] = gw2[0 : second_kernel.shape[0]].astype(float_type)
    rows, channels = output_weight.shape
    for n in range(3):
        joint_weight[:, n * channels : (n + 1) * channels] = go[n * rows : (n + 1) * rows].astype(
            float_type
        )
    output_weight[...] = go[3 * rows :].astype(float_type)

    def own(v, size, place):
        width = v.shape[1]
        return pltpu.roll(v, lax.rem(width - place * size, width), 1)

    late = own(gv[1], rows, r)
    early = own(gv[0], rows, r)
    for n, ref in enumerate((first_gain, first_shift, first_offset)):
        ref[...] = late[n, 0:rows]
    for n, ref in (
        (3, second_gain), (4, second_shift), (5, second_offset), (6, third_gain),
        (7, third_shift), (10, output_offset),
    ):
        ref[...] = early[n, 0:rows]
    pair = own(gv[0], 2 * rows, lax.rem(r, 2))
    joint_offset[...] = jnp.where(r < 2, pair[8:9, 0 : 2 * rows], pair[9:10, 0 : 2 * rows]).reshape(
        2 * rows
    )
    embed_offset[...] = own(geo[...], 2 * rows, r)[0, 0 : 2 * rows]
    for cp in moves:
        cp.wait()


def finish_call(res, gx, gw1, gw2, go, gv, ge, gc, geo):
    channels = go.shape[0]
    rows = channels // 4
    vm = pl.BlockSpec(memory_space=pltpu.VMEM)
    hbm = pl.BlockSpec(memory_space=pl.ANY)

    def out(*shape, kind=float_type):
        return jax.ShapeDtypeStruct(shape, kind)

    kernel = out(9 * rows, channels)
    line = out(rows)
    return pl.pallas_call(
        finish_kernel,
        out_shape=(
            out(*res.shape, kind=low_type), out(*gx.shape), line, line, kernel, line,
            out(*ge.shape), out(2 * rows), out(*gc.shape), line, line, kernel, line, line, line,
            out(rows, 3 * channels), out(2 * rows), out(rows, channels), line,
        ),
        in_specs=[hbm, hbm, vm, vm, vm, vm, hbm, hbm, vm],
        out_specs=(hbm, hbm, vm, vm, vm, vm, hbm, vm, hbm) + (vm,) * 10,
        scratch_shapes=[pltpu.SemaphoreType.DMA((4,))],
        compiler_params=pltpu.CompilerParams(vmem_limit_bytes=32 << 20),
        name="finish",
    )(res, gx, gw1, gw2, go, gv, ge, gc, geo)


def shards(
    images,
    level_count,
    level_index,
    labels,
    first_gain,
    first_shift,
    first_kernel,
    first_offset,
    embed_weight,
    embed_offset,
    class_table,
    second_gain,
    second_shift,
    second_kernel,
    second_offset,
    third_gain,
    third_shift,
    joint_weight,
    joint_offset,
    output_weight,
    output_offset,
    cotangent,
):
    image_count, stripe_rows, image_width, channels = images.shape
    pixels = stripe_rows * image_width
    x = images.reshape(image_count, pixels, channels)
    cot = cotangent.reshape(image_count, pixels, channels)
    lines = (
        first_gain, first_shift, first_offset, second_gain, second_shift, second_offset,
        third_gain, third_shift, joint_offset, output_offset, embed_offset,
    )
    found = block_call(
        x, cot, lines, (level_count, level_index, labels), first_kernel, second_kernel,
        joint_weight, output_weight, embed_weight, class_table,
    )
    outs = finish_call(*found)
    return (outs[0].reshape(images.shape), outs[1].reshape(images.shape)) + tuple(outs[2:])


def solution(mesh):
    in_specs = (
        (P("img", "row", None, None),) + (P("img"),) * 3 + (P(),) * 17
        + (P("img", "row", None, None),)
    )
    row, rows = P("row"), P("row", None)
    out_specs = (
        P("img", "row", None, None), P("img", "row", None, None), row, row, rows, row, rows, row,
        rows, row, row, rows, row, row, row, rows, row, rows, row,
    )
    return jax.shard_map(shards, mesh=mesh, in_specs=in_specs, out_specs=out_specs, check_vma=False)
```

profile of v0, /device:TPU:0, one launch (start us, length us, event | category | flops | bytes accessed | tf_op | source)
XLA Modules:
  0.0 159.5 jit_solution(5572382071310970299)
XLA Ops:
  0.7 146.0 %block.1 = (bf16[3,256,384]{2,1,0:T(8,128)(2,1)}, f32[3,256,384]{2,1,0:T(8,128)}, bf16[896,384]{1,0:T(8,128)(2,1)}, bf16[896,384]{1,0:T(8,128)(2,1)}, bf16[384,3...) custom-call(bf16[3,256,384]{2,1,0:T(8,128)(2,1)} %bitcast.4, ...), custom_call_target="tpu_custom_call" | custom-call | tf_op jit(solution)/shard_map/block/pallas_call | solution.py:1028
  146.7 0.0 copy-start
  146.7 1.3 copy-done
  148.0 0.0 copy-start.1
  148.0 1.1 copy-done.1
  149.1 0.0 copy-start.2
  149.1 1.1 copy-done.2
  150.2 0.0 copy-start.3
  150.2 1.1 copy-done.3
  151.3 0.0 copy-start.4
  151.3 1.1 copy-done.4
  152.4 0.0 copy-start.5
  152.4 1.1 copy-done.5
  153.4 0.0 copy-start.6
  153.4 1.0 copy-done.6
  154.4 0.0 copy-start.7
  154.4 0.8 copy-done.7
  155.2 0.0 copy-start.8
  155.2 0.7 copy-done.8
  155.9 3.4 %finish.1 = (bf16[3,256,384]{2,1,0:T(8,128)(2,1)}, f32[3,256,384]{2,1,0:T(8,128)}, f32[96]{0:T(128)}, f32[96]{0:T(128)}, f32[864,384]{1,0:T(8,128)}, /*index=5*/...) custom-call(bf16[3,256,384]{2,1,0:T(8,128)(2,1)S(1)} %copy-done.4, ...), custom_call_target="tpu_custom_call" | custom-call | tf_op jit(solution)/shard_map/finish/pallas_call | solution.py:1132
Async XLA Ops:
  146.7 1.3 copy-start
  148.0 1.1 copy-start.1
  149.1 1.1 copy-start.2
  150.2 1.1 copy-start.3
  151.3 1.1 copy-start.4
  152.4 1.1 copy-start.5
  153.4 1.0 copy-start.6
  154.4 0.8 copy-start.7
  155.2 0.7 copy-start.8
where the time goes:
time: 160 us
  Pallas kernels  149 us (93%)
  local copies, waits for them, and re-layouts  9.22 us (6%)
    pallas_call x1, Pallas kernels, block_call(): pl.pallas_call(block_kernel, out_shape=(out(*x.shape, kind=low_type), out...  146 us
    unnamed x18, local copies, waits for them, and re-layouts  9.22 us
    pallas_call x1, Pallas kernels, finish_call(): pl.pallas_call(finish_kernel, out_shape=(out(*res.shape, kind=low_type),...  3.42 us

commit v1 on v0

--- a/solution.py
+++ b/solution.py
@@ -214,16 +214,34 @@
             cp.wait_send()
 
 
+def out_rows(pixels, channels, classes):
+    def laid(sizes):
+        found, at = {}, 0
+        for name, size in sizes:
+            found[name] = (at, size)
+            at += size
+        return found
+
+    padded = -(-9 * channels // 4 // 128) * 128
+    rows = -(-classes // 4 // 16) * 16
+    low_at = laid((("result", pixels), ("w1", padded), ("w2", padded), ("jo", channels)))
+    wide_at = laid((
+        ("images", pixels), ("lines", 32), ("embed", channels), ("classes", 2 * rows),
+        ("offset", 16),
+    ))
+    return low_at, wide_at
+
+
 def block_kernel(
     x_ref, cot_ref, *rest,
 ):
     lines, rest = rest[:11], rest[11:]
     count_ref, index_ref, label_ref = rest[:3]
     (w1_any, w2_any, jw_any, ow_any, ew_any, ct_any,
-    res_ref, gx_ref, gw1_ref, gw2_ref, go_ref, gv_ref, ge_ref, gc_ref, geo_ref,
+    low_out, wide_out,
     w1, w2, jw, ow, ew, ct, ones, hid, mid, mod, emb, act1_t, act2_t, st, m1, m3, got,
     att, att_t, kv, kv_t, q8, d_out_t, qm, dom, s_ref, eb, dsb, mix_t, dq_t, dq, dkv,
-    got_core, got_x, ag, q_sum, kv_sum, o_sum, gjo,
+    got_core, to_x, got_x, ag, q_sum, kv_sum, o_sum, gjo,
     grad, slope_grad, gs, mg,
     gw, w_core, w_got_x, w_own, w_got_y, w_got_z, w_got_e,
     o_core, o_got_x, o_own, o_got_y, o_got_z, o_got_e,
@@ -265,6 +283,11 @@
         pl.semaphore_signal(barrier, inc=1, device_id=at, device_id_type=MESH)
 
     abuf = grad.at[0]
+    low_at, wide_at = out_rows(images * pixels, channels, ct.shape[0])
+    gw1_ref, gw2_ref, go_ref = (low_out.at[pl.ds(*low_at[n])] for n in ("w1", "w2", "jo"))
+    gv_ref, ge_ref, gc_ref, geo_ref = (
+        wide_out.at[pl.ds(*wide_at[n])] for n in ("lines", "embed", "classes", "offset")
+    )
 
     def dot(a, b):
         return jnp.dot(a, b, preferred_element_type=float_type)
@@ -305,7 +328,7 @@
     def each_image(step):
         some_images(step, 0, images)
 
-    message_rows = (48, 48, 48, 48, 48, 16, 48)
+    message_rows = (48, 48, 48, 16, 48, 16, 48)
 
     def copies(p, b):
         full, stat = pl.ds(0, message_rows[p]), pl.ds(0, 16)
@@ -427,7 +450,18 @@
 
     def small_y(s):
         arrived(small_row_copies(s))
-        v_one[s] = v_own[s] + v_row[s, 0] + v_row[s, 1] + v_row[s, 2]
+        v = v_own[s] + v_row[s, 0] + v_row[s, 1] + v_row[s, 2]
+        quarter_of = channels // 4
+        v = pltpu.roll(v, lax.rem(channels - r * quarter_of, channels), 1)
+        v_one[s] = v[:, 0:128]
+        if s == 0:
+            double = lax.rem(r, 2) * 2 * quarter_of
+            pair = jnp.where(r < 2, v_own[0, 8:9], v_own[0, 9:10])
+            for k in range(3):
+                pair = pair + jnp.where(r < 2, v_row[0, k, 8:9], v_row[0, k, 9:10])
+            pair = pltpu.roll(pair, lax.rem(channels - double, channels), 1)
+            v_one[0, 8:9] = pair[:, 0:128]
+            v_one[0, 9:10] = pltpu.roll(pair, channels - 128, 1)[:, 0:128]
         start(small_y_copies(s))
 
     def small_z(s):
@@ -444,7 +478,7 @@
             arrived(small_e_copies(s))
             for n in range(len(extras)):
                 total = total + v_e[s, n]
-        gv_ref[s] = total
+        gv_ref[pl.ds(16 * s, 16), 0:128] = total
 
     def gather_row_copies():
         return [
@@ -459,15 +493,21 @@
         for rows, places in zip(blocks, (chips["y"], zs, extras)):
             for at in places:
                 n = 3 + len(found)
-                found.append(remote(gat.at[rows], gat.at[rows], gsem.at[n], hsem.at[n], at))
+                part_of = gat.at[c, rows]
+                found.append(remote(part_of, part_of, gsem.at[n], hsem.at[n], at))
         return found
+
+    def gather_core_copies():
+        n = 7 + len(extras)
+        return [remote(gat.at[c], gat.at[c], gsem.at[n], hsem.at[n], who[1])]
 
     def gather_row():
         start(gather_row_copies())
 
     def gather_y():
         arrived(gather_row_copies())
-        gat[i] = emb[...] + mg[...] + g_row[0] + g_row[1] + g_row[2]
+        v = emb[...] + mg[...] + g_row[0] + g_row[1] + g_row[2]
+        gat[c, i] = jnp.where(c == 0, v[:, :channels], v[:, channels:])
         start(gather_copies()[:1])
 
     def gather_z():
@@ -478,6 +518,12 @@
         arrived(gather_copies()[1:4])
         start(gather_copies()[4:])
         arrived(gather_copies()[4:])
+        start(gather_core_copies())
+
+    def gather_core():
+        other = gat.at[1 - c]
+        n = 7 + len(extras)
+        remote(other, other, gsem.at[n], hsem.at[n], who[1]).wait_recv()
 
     def three_terms(v):
         a = v.astype(low_type)
@@ -486,14 +532,16 @@
         return jnp.concatenate([a, b, d], axis=0)
 
     def embedding():
-        ge_ref[...] = jnp.zeros(ge_ref.shape, float_type)
-        gc_ref[...] = jnp.zeros(gc_ref.shape, float_type)
-        geo_ref[...] = jnp.zeros(geo_ref.shape, float_type)
-        lax.fori_loop(0, gat.shape[0] // 8, embedding_part, 0)
+        for ref in (ge_ref, gc_ref, geo_ref):
+            ref[...] = jnp.zeros(ref.shape, float_type)
+        lax.fori_loop(0, gat.shape[1] // 8, embedding_part, 0)
 
     def embedding_part(part_of, _):
         every = 64
-        full = gat[pl.ds(pl.multiple_of(part_of * 8, 8), 8)].reshape(every, 2 * channels)
+        groups = pl.ds(pl.multiple_of(part_of * 8, 8), 8)
+        full = jnp.concatenate(
+            [gat[n, groups].reshape(every, channels) for n in range(2)], axis=1
+        )
         place_of = lax.rem(lax.broadcasted_iota(jnp.int32, (every, 2 * channels), 0), 8)
         live = place_of < images
         grad = jnp.where(live, full, 0.0)
@@ -503,12 +551,16 @@
         terms = three_terms(grad)
         size = 2 * channels // 4
         own = pl.ds(pl.multiple_of(r * size, size), size)
-        ge_ref[...] += jnp.dot(left[own, :], terms, preferred_element_type=float_type)
-        geo_ref[...] += jnp.broadcast_to(jnp.sum(grad, axis=0, keepdims=True), geo_ref.shape)
+        v = jnp.dot(left[own, :], terms, preferred_element_type=float_type)
+        ge_ref[0:size] += v[:, :channels]
+        ge_ref[size : 2 * size] += v[:, channels:]
+        v = jnp.sum(grad, axis=0, keepdims=True)
+        geo_ref[0:1] += v[:, :channels]
+        geo_ref[8:9] += v[:, channels:]
         active = lax.dot_general(terms, ew[...], contract_cols, preferred_element_type=float_type)
         active = active[0:every] + active[every : 2 * every] + active[2 * every :]
         back = jnp.where(live, active * slope_of(held), 0.0)
-        classes = gc_ref.shape[0]
+        classes = ct.shape[0] // 4
         row_of = lax.rem(lax.broadcasted_iota(jnp.int32, (every, 128), 0), 8)
         label = jnp.full((every, 128), -1.0, float_type)
         for b in range(images):
@@ -519,7 +571,9 @@
             hit = jnp.where(label == kind.astype(float_type), 1.0, 0.0).astype(low_type)
             hot[128 * n : 128 * (n + 1), :] = jnp.concatenate([hit, hit, hit], axis=0).T
         found = jnp.dot(hot[...], three_terms(back), preferred_element_type=float_type)
-        gc_ref[...] += found[0:classes]
+        height = gc_ref.shape[0] // 2
+        gc_ref[0:height] += found[0:height, :channels]
+        gc_ref[height:] += found[0:height, channels:]
         return 0
 
     def embed_forward():
@@ -600,10 +654,7 @@
     def _(b):
         d_out_t[b] = dot_nt(cot_ref[b], ow[...]).T.astype(low_type)
 
-    loads["w1"].wait()
-
-    @each_image
-    def _(b):
+    def first_convolution(b):
         centre, scaled = receive_scale(0, b)
         slope = scaled * vec(0)
         shift = vec(1)
@@ -625,6 +676,12 @@
         act1_t[:, own] = abuf[width : width + pixels, channels : 2 * channels].T
 
     def block(n):
+        return pl.ds(pl.multiple_of(width + n * pixels, width), pixels)
+
+    def wide_block(n):
+        return pl.ds(pl.multiple_of(n * pixels, width), pixels + 2 * width)
+
+    def span_of(n):
         return pl.ds(pl.multiple_of(n * pixels, pixels), pixels)
 
     mate = r + 1 - 2 * c
@@ -648,15 +705,7 @@
         att[b, block(r)] = ((mid[b] - centre) * slope + vec(7)).astype(low_type)
         start(shares(b)[:2])
 
-    loads["w2"].wait()
-    loads["jw"].wait()
-
-    @each_image
-    def _(b):
-        @pl.when(b == images - 1)
-        def _():
-            share(0)
-
+    def second_convolution(b):
         centre, scaled = receive_scale(1, b)
         grow = 1.0 + mod[pl.ds(b, 1), 0:channels]
         slope = scaled * vec(3) * grow
@@ -678,6 +727,15 @@
         own = pl.ds(pl.multiple_of(b * pixels, pixels), pixels)
         act2_t[:, own] = abuf[width : width + pixels, channels : 2 * channels].T
 
+    loads["w1"].wait()
+    loads["w2"].wait()
+    loads["jw"].wait()
+    some_images(first_convolution, 0, 2)
+    some_images(second_convolution, 0, 1)
+    some_images(first_convolution, 2, images)
+    share(0)
+    some_images(second_convolution, 1, images)
+
     part = att
 
     def forward(b):
@@ -687,33 +745,35 @@
     def sums_core(b):
         return [
             remote(
-                part.at[b, block(2 * n + 1 - c)], got_core.at[b, n], asem.at[b, n],
+                part.at[b, wide_block(2 * n + 1 - c)], got_core.at[b, n], asem.at[b, n],
                 bsem.at[b, n], who[1],
             )
             for n in range(2)
         ]
 
     def sum_x(b):
-        far = block(2 * (1 - lax.div(r, 2)) + c)
-        return remote(part.at[b, far], got_x.at[b], asem.at[b, 2], bsem.at[b, 2], who[2])
+        return remote(to_x, got_x.at[b], asem.at[b, 2], bsem.at[b, 2], who[2])
 
     def pass_on(b):
         x = lax.div(r, 2)
         arrived(sums_core(b))
+
+        @pl.when(b > 0)
+        def _():
+            sum_x(b - 1).wait_send()
+
         far = 1 - x
-        rows = block(2 * far + c)
-        part[b, rows] = (
-            part[b, rows].astype(float_type) + got_core[b, far].astype(float_type)
+        to_x[...] = (
+            part[b, wide_block(2 * far + c)].astype(float_type)
+            + got_core[b, far].astype(float_type)
         ).astype(low_type)
         sum_x(b).start()
-        ag[b] = part[b, block(r)].astype(float_type) + got_core[b, x].astype(float_type)
+        ag[b] = part[b, wide_block(r)].astype(float_type) + got_core[b, x].astype(float_type)
 
     def queries(b):
         q = (dot(att[b, block(r)], jw[:, :channels]) + vec(8)).astype(low_type)
-        q8[b] = (q.astype(float_type) * HEAD ** (-0.5)).astype(low_type)
-
-    some_images(share, 1, images)
-    each_image(queries)
+        q8[...] = (q.astype(float_type) * HEAD ** (-0.5)).astype(low_type)
+
     lane = lax.broadcasted_iota(jnp.int32, (pixels, pair_lanes), 1)
 
     def masked(v):
@@ -725,17 +785,36 @@
     kv_sum[...] = jnp.zeros(kv_sum.shape, float_type)
     o_sum[...] = jnp.zeros(o_sum.shape, float_type)
     att_t[channels:] = jnp.ones((16, whole), low_type)
-    forward(0)
+    none = jnp.zeros((width, channels), low_type)
+    for b in range(images):
+        att[b, 0:width] = none
+        att[b, width + whole :] = none
 
     @each_image
     def _(b):
         a = arrivals(b)
+        bias = jnp.concatenate([jnp.zeros((1, channels), float_type), vec(9)], axis=1)
+
+        def project(x):
+            rows = pl.ds(pl.multiple_of(width + 2 * x * pixels, width), 2 * pixels)
+            to = pl.ds(pl.multiple_of(2 * x * pixels, 2 * pixels), 2 * pixels)
+            kv[to] = (dot(att[b, rows], jw[:, channels:]) + bias).astype(low_type)
+
+        queries(b)
         a[0].wait_recv()
+        project(lax.div(r, 2))
+
+        @pl.when(b == 0)
+        def _():
+            forward(0)
+
         a[2].wait_recv()
-        bias = jnp.concatenate([jnp.zeros((1, channels), float_type), vec(9)], axis=1)
-        for n in range(4):
-            rows = pl.ds(n * pixels, pixels)
-            kv[rows] = (dot(att[b, rows], jw[:, channels:]) + bias).astype(low_type)
+        project(1 - lax.div(r, 2))
+
+        @pl.when(b == 0)
+        def _():
+            some_images(share, 1, images)
+
         for n in range(2 * channels // 128):
             cols = pl.ds(n * 128, 128)
             kv_t[cols, :] = kv[:, cols].T
@@ -747,7 +826,7 @@
         def one_pair(t, _):
             lanes = pl.ds(pl.multiple_of(t * pair_lanes, pair_lanes), pair_lanes)
             v_lanes = pl.ds(pl.multiple_of(channels + t * pair_lanes, pair_lanes), pair_lanes)
-            qm[...] = masked(q8[b, :, lanes].astype(float_type))
+            qm[...] = masked(q8[:, lanes].astype(float_type))
             peak = None
             for n in range(whole // chunk):
                 rows = pl.ds(n * chunk, chunk)
@@ -795,21 +874,33 @@
             forward(b + 1)
 
         dq[...] = dq_t[...].T.astype(low_type)
-        att_t[0:channels] = att[b].T
+        att_t[0:channels] = att[b, width : width + whole].T
         for cp in shares(b):
             cp.wait_send()
+        own = dot_nt(dq[...], jw[:, :channels])
+        first = col_sum(own)
+        second = col_sum(own * att[b, block(r)].astype(float_type))
         for n in range(4):
-            rows = pl.ds(n * pixels, pixels)
-            part[b, rows] = dot_nt(dkv[rows], jw[:, channels:]).astype(low_type)
-        part[b, block(r)] = (
-            part[b, block(r)].astype(float_type) + dot_nt(dq[...], jw[:, :channels])
-        ).astype(low_type)
+            rows = pl.ds(width + n * pixels, pixels)
+            v = dot_nt(dkv[n * pixels : (n + 1) * pixels], jw[:, channels:])
+            first += col_sum(v)
+            second += col_sum(v * att[b, rows].astype(float_type))
+            part[b, rows] = v.astype(low_type)
+        part[b, block(r)] = (part[b, block(r)].astype(float_type) + own).astype(low_type)
         start(sums_core(b))
-        q_sum[...] += dot(att_t[:, block(r)], dq[...])
+        second = (second - vec(7) * first) / vec(6)
+        gs[6:7] += second
+        gs[7:8] += first
+        send(3, b, first * vec(6), second * vec(6))
+        q_sum[...] += dot(att_t[:, span_of(r)], dq[...])
         kv_sum[...] += dot(att_t[...], dkv[...])
+
+        @pl.when(b == images - 1)
+        def _():
+            pass_on(b)
+
         o_sum[...] += dot(mix_t[...], cot_ref[b])
-        mixed = mix_t[...].T
-        res_ref[b] = (mid[b] + dot(mixed, ow[...]) + vec(10)).astype(low_type)
+        low_out[span_of(b)] = mix_t[...].T
 
     def pack_weights():
         part_rows = channels // 4
@@ -823,37 +914,32 @@
         gs[9:10] = kv_sum[channels : channels + 1, channels:]
         gs[10:11] = col_sum(jnp.sum(cot_ref[...].astype(float_type), axis=0))
 
-    def attend_sums(b):
-        sum_x(b).wait_recv()
-        u = ag[b] + got_x[b].astype(float_type)
-        ag[b] = u
-        first = col_sum(u)
-        second = col_sum(u * ((mid[b] - st[b, 4:5]) * st[b, 5:6]))
-        gs[6:7] += second
-        gs[7:8] += first
-        send(3, b, first * vec(6), second * vec(6), lambda at: ag[b, pl.ds(at, width)])
+    def result(b):
+        v = mid[b] + dot(low_out[span_of(b)], ow[...]) + vec(10)
+        low_out[span_of(b)] = v.astype(low_type)
 
     def branch_grad(b):
         first, second = receive(3, b)
         arrived(copies(6, b))
+        sum_x(b).wait_recv()
         centre, scaled = st[b, 4:5], st[b, 5:6]
 
-        def grad_of(cot, u, v):
+        def grad_of(cot, rows, v):
+            u = ag[b, rows] + got_x[b, rows].astype(float_type)
             return (cot + scaled * (u * vec(6) - first - (v - centre) * scaled * second)) * half
 
         total = jnp.zeros((1, channels), float_type)
         for row in range(rows_in):
             rows = pl.ds(row * width, width)
-            v = grad_of(cot_ref[b, rows].astype(float_type), ag[b, rows], mid[b, rows])
-            ag[b, rows] = v
+            inside = pl.ds((row + 1) * width, width)
+            v = grad_of(cot_ref[b, rows].astype(float_type), inside, mid[b, rows])
+            ag[b, inside] = v
             v = v.astype(low_type).astype(float_type)
             fill_row(grad.at[b], (row + 1) * width, v, channels, width)
             total += col_sum(v)
         gs[5:6] += total
-        fill_halo(
-            grad.at[b],
-            lambda k: grad_of(far_rows(6, b, k), far_rows(3, b, k), far_rows(2, b, k)),
-        )
+        places = {0: pl.ds(inner_halo, width), 2: pl.ds(outer_halo, width)}
+        fill_halo(grad.at[b], lambda k: grad_of(far_rows(6, b, k), places[k], far_rows(2, b, k)))
 
     def branch_back(b):
         upstream = data_grad(grad, b, w2)
@@ -904,100 +990,102 @@
         first, second = receive(5, b)
         scaled = st[b, 1:2]
         normed = (x_ref[b].astype(float_type) - st[b, 0:1]) * scaled
-        gx_ref[b] = ag[b] + scaled * (slope_grad[b] * vec(0) - first - normed * second)
-
-    pass_on(images - 1)
-    some_images(attend_sums, 0, images - 1)
+        v = scaled * (slope_grad[b] * vec(0) - first - normed * second)
+        wide_out[span_of(b)] = ag[b, width : width + pixels] + v
+
     pack_weights()
+    some_images(branch_grad, 0, images - 1)
     red0.core()
-    some_images(attend_sums, images - 1, images)
     red0.across_x()
-    some_images(branch_grad, 0, images - 1)
     some_images(branch_back, 0, images - 1)
     some_images(branch_grad, images - 1, images)
-    kernel_grad(act2_t, grad, 0)
-    red2[1].core()
     some_images(branch_back, images - 1, images)
     small_row(0)
     gather_row()
+    kernel_grad(act2_t, grad, 0)
+    red2[0].core()
     red0.across_y()
+    red2[1].core()
+    red2[2].core()
+    red2[0].across_x()
+    each_image(result)
     some_images(hidden_grad, 0, images - 1)
+    red2[2].across_x()
     red2[1].across_x()
-    red2[0].core()
-    red2[2].core()
-    some_images(hidden_grad, images - 1, images)
-    red2[0].across_x()
-    kernel_grad(act1_t, grad, 3)
-    red0.across_z()
     small_y(0)
     gather_y()
-    red1[1].core()
-    red2[2].across_x()
-    red1[0].core()
-    red1[2].core()
-    some_images(hidden_back, 0, images - 1)
-    red1[0].across_x()
-    red1[1].across_x()
-    red2[1].across_y()
-    some_images(hidden_back, images - 1, images)
-    red1[2].across_x()
+    some_images(hidden_grad, images - 1, images)
+    red0.across_z()
+    red2[0].across_y()
     small_z(0)
     gather_z()
-    small_row(1)
+    kernel_grad(act1_t, grad, 3)
+    red1[2].core()
     red0.back_z()
-    red2[0].across_y()
+    red1[0].core()
+    red2[0].across_z()
+    red1[2].across_x()
+    red2[2].across_y()
+    red1[1].core()
+    red2[1].across_y()
+    red2[2].across_z()
+    red1[1].across_x()
+    red1[0].across_x()
+    some_images(hidden_back, images - 1, images)
+    red2[0].back_z()
+    red1[2].across_y()
     red2[1].across_z()
+    red2[2].back_z()
+    some_images(hidden_back, 0, images - 1)
+    red1[1].across_y()
     small_end(0)
     gather_end()
+    red1[2].across_z()
+    red2[0].back_y()
+    red2[1].back_z()
+    red1[0].across_y()
+    red0.back_y()
+    red1[1].across_z()
+    small_row(1)
+    red2[2].back_y()
+    each_image(images_grad)
+    red2[0].end()
+    red1[2].back_z()
+    red1[0].across_z()
+    red1[1].back_z()
+    red1[2].back_y()
+    gather_core()
     embedding()
-    red2[2].across_y()
-    red0.back_y()
-    red2[0].across_z()
-    red2[1].back_z()
-    red2[2].across_z()
-    red1[0].across_y()
-    red2[0].back_z()
+    red1[0].back_z()
     red2[1].back_y()
+    small_y(1)
+    red1[1].back_y()
+    red1[0].back_y()
+    red2[2].end()
     red0.end()
-    red1[1].across_y()
-    red2[2].back_z()
-    each_image(images_grad)
-    red1[0].across_z()
-    red2[0].back_y()
+    red1[2].end()
+    small_z(1)
+    small_end(1)
+    red1[1].end()
     red2[1].end()
-    red1[2].across_y()
-    red1[1].across_z()
-    red2[2].back_y()
-    small_y(1)
-    red2[0].end()
-    red1[0].back_z()
-    red1[2].across_z()
-    red1[1].back_z()
-    red2[2].end()
-    red1[0].back_y()
-    small_z(1)
-    red1[2].back_z()
-    red1[1].back_y()
     red1[0].end()
-    small_end(1)
-    red1[2].back_y()
-    red1[1].end()
-    red1[2].end()
 
     @each_image
     def _(b):
-        sent = sums_core(b) + [sum_x(b)]
+        sent = sums_core(b)
         for p in range(7):
             sent += copies(p, b)
         for cp in sent:
             cp.wait_send()
+
+    sum_x(images - 1).wait_send()
 
     for red in [red0] + red1 + red2:
         red.drain()
     for s in range(2):
         for cp in small_row_copies(s) + small_y_copies(s) + small_z_copies(s) + small_e_copies(s):
             cp.wait_send()
-    for cp in gather_row_copies() + gather_copies():
+    for cp in gather_row_copies() + gather_copies() + gather_core_copies():
         cp.wait_send()
 
 
@@ -1009,7 +1097,7 @@
     every = lax.axis_size("img")
     more = every // 8
     some = max(more - 1, 1)
-    classes = ct.shape[0]
+    low_at, wide_at = out_rows(images * pixels, channels, ct.shape[0])
     vm = pl.BlockSpec(memory_space=pltpu.VMEM)
     hbm = pl.BlockSpec(memory_space=pl.ANY)
 
@@ -1028,13 +1116,10 @@
     return pl.pallas_call(
         block_kernel,
         out_shape=(
-            out(*x.shape, kind=low_type), out(*x.shape), out(padded, channels, kind=low_type),
-            out(padded, channels, kind=low_type), out(channels, channels, kind=low_type),
-            out(2, 16, channels), out(2 * channels // 4, 2 * channels),
-            out(classes // 4, 2 * channels), out(8, 2 * channels),
+            out(sum(low_at["jo"]), channels, kind=low_type), out(sum(wide_at["offset"]), channels),
         ),
         in_specs=[vm] * (2 + len(lines)) + [pl.BlockSpec(memory_space=pltpu.SMEM)] * 3 + [hbm] * 6,
-        out_specs=(vm,) * 9,
+        out_specs=(vm,) * 2,
         scratch_shapes=[
             low(*w1.shape), low(*w2.shape), low(*jw.shape), low(*ow.shape), low(*ew.shape),
             low(*ct.shape), low(channels, channels), wide(*x.shape), wide(*x.shape),
@@ -1042,12 +1127,13 @@
             low(channels, images * pixels), low(channels, images * pixels),
             wide(images, 8, channels), low(7, images, 48, channels), low(7, images, 48, channels),
             low(7, images, 3, 48, channels),
-            low(images, whole, channels), low(channels + 16, whole), low(whole, 2 * channels),
-            low(2 * channels, whole), low(*x.shape), low(images, channels, pixels),
+            low(images, whole + 64, channels), low(channels + 16, whole), low(whole, 2 * channels),
+            low(2 * channels, whole), low(pixels, channels), low(images, channels, pixels),
             low(2 * pixels, 2 * HEAD), low(2 * pixels, 2 * HEAD), wide(whole, 2 * pixels),
             low(whole, 2 * pixels), low(whole, 2 * pixels), low(channels, pixels),
             wide(channels, pixels), low(pixels, channels), low(whole, 2 * channels),
-            low(images, 2, pixels, channels), low(*x.shape), wide(*x.shape),
+            low(images, 2, span, channels), low(span, channels), low(images, span, channels),
+            wide(images, span, channels),
             wide(channels + 16, channels),
             wide(channels + 16, 2 * channels), wide(channels, channels), low(4, channels, channels),
             low(images, span, 3 * channels), wide(*x.shape), wide(16, channels), wide(8, 2 * channels),
@@ -1057,13 +1143,13 @@
             low(2, channels, channels), low(channels, channels), wide(channels // 2, channels),
             low(channels // 2, channels), low(3, channels // 8, channels),
             low(some, channels // 8, channels),
-            wide(2, 16, channels), wide(2, 3, 16, channels), wide(2, 16, channels),
-            wide(2, 16, channels), wide(2, 16, channels), wide(2, 3, 16, channels),
-            wide(2, 16, channels), wide(2, some, 16, channels), wide(3, 8, 2 * channels),
-            wide(every, 8, 2 * channels), low(2 * channels, 192), low(256, 192), wide(16, channels), wide(8, 2 * channels),
+            wide(2, 16, channels), wide(2, 3, 16, channels), wide(2, 16, 128),
+            wide(2, 16, 128), wide(2, 16, 128), wide(2, 3, 16, 128), wide(2, 16, 128),
+            wide(2, some, 16, 128), wide(3, 8, 2 * channels), wide(2, every, 8, channels),
+            low(2 * channels, 192), low(256, 192), wide(16, channels), wide(8, 2 * channels),
             dma(6), dma(7, images, 3), dma(7, images, 3), dma(images, 3), dma(images, 3),
             dma(images, 3), dma(images, 3), dma(7, 11), dma(7, 11), dma(7, some), dma(7, some),
-            dma(2, 6 + more), dma(2, 6 + more), dma(6 + more), dma(6 + more),
+            dma(2, 6 + more), dma(2, 6 + more), dma(7 + more), dma(7 + more),
         ],
         compiler_params=pltpu.CompilerParams(
             collective_id=0, has_side_effects=True, vmem_limit_bytes=62 << 20
@@ -1073,53 +1159,69 @@
 
 
 def finish_kernel(
-    res, gx, gw1, gw2, go, gv, ge, gc, geo,
-    res_out, gx_out, first_gain, first_shift, first_kernel, first_offset, embed_weight,
+    low_any, wide_any,
+    result, images, first_gain, first_shift, first_kernel, first_offset, embed_weight,
     embed_offset, class_table, second_gain, second_shift, second_kernel, second_offset,
-    third_gain, third_shift, joint_weight, joint_offset, output_weight, output_offset, sems,
+    third_gain, third_shift, joint_weight, joint_offset, output_weight, output_offset,
+    low_in, wide_in, sems,
 ):
     r = lax.axis_index("row")
+    rows, channels = output_weight.shape
+    pixels = result.shape[0]
+    low_at, wide_at = out_rows(pixels, channels, 4 * class_table.shape[0])
     moves = [
         pltpu.make_async_copy(src, dst, sems.at[n])
-        for n, (src, dst) in enumerate(
-            ((res, res_out), (gx, gx_out), (ge, embed_weight), (gc, class_table))
-        )
+        for n, (src, dst) in enumerate((
+            (low_any, low_in), (wide_any, wide_in), (low_in.at[pl.ds(0, pixels)], result),
+            (wide_in.at[pl.ds(0, pixels)], images),
+        ))
     ]
-    for cp in moves:
-        cp.start()
-    first_kernel[...] = gw1[0 : first_kernel.shape[0]].astype(float_type)
-    second_kernel[...] = gw2[0 : second_kernel.shape[0]].astype(float_type)
-    rows, channels = output_weight.shape
+    moves[0].start()
+    moves[1].start()
+
+    def low_rows(name, start, size):
+        at = low_at[name][0] + start
+        return low_in[at : at + size].astype(float_type)
+
+    def wide_rows(name, start, size):
+        at = wide_at[name][0] + start
+        return wide_in[at : at + size]
+
+    moves[0].wait()
+    moves[2].start()
+    first_kernel[...] = low_rows("w1", 0, 9 * rows)
+    second_kernel[...] = low_rows("w2", 0, 9 * rows)
     for n in range(3):
-        joint_weight[:, n * channels : (n + 1) * channels] = go[n * rows : (n + 1) * rows].astype(
-            float_type
-        )
-    output_weight[...] = go[3 * rows :].astype(float_type)
-
-    def own(v, size, place):
-        width = v.shape[1]
-        return pltpu.roll(v, lax.rem(width - place * size, width), 1)
-
-    late = own(gv[1], rows, r)
-    early = own(gv[0], rows, r)
-    for n, ref in enumerate((first_gain, first_shift, first_offset)):
-        ref[...] = late[n, 0:rows]
+        joint_weight[:, n * channels : (n + 1) * channels] = low_rows("jo", n * rows, rows)
+    output_weight[...] = low_rows("jo", 3 * rows, rows)
+    moves[1].wait()
+    moves[3].start()
+    lines = wide_rows("lines", 0, 32)
     for n, ref in (
-        (3, second_gain), (4, second_shift), (5, second_offset), (6, third_gain),
-        (7, third_shift), (10, output_offset),
+        (16, first_gain), (17, first_shift), (18, first_offset), (3, second_gain),
+        (4, second_shift), (5, second_offset), (6, third_gain), (7, third_shift),
+        (10, output_offset),
     ):
-        ref[...] = early[n, 0:rows]
-    pair = own(gv[0], 2 * rows, lax.rem(r, 2))
-    joint_offset[...] = jnp.where(r < 2, pair[8:9, 0 : 2 * rows], pair[9:10, 0 : 2 * rows]).reshape(
-        2 * rows
-    )
-    embed_offset[...] = own(geo[...], 2 * rows, r)[0, 0 : 2 * rows]
-    for cp in moves:
+        ref[...] = lines[n, 0:rows]
+    joint_offset[...] = jnp.concatenate([lines[8:9, 0:128], lines[9:10, 0:128]], axis=1)[
+        0, 0 : 2 * rows
+    ]
+    size = 2 * rows
+    classes = class_table.shape[0]
+    reach = wide_at["classes"][1] // 2
+    for n in range(2):
+        cols = slice(n * channels, (n + 1) * channels)
+        embed_weight[:, cols] = wide_rows("embed", n * size, size)
+        class_table[:, cols] = wide_rows("classes", n * reach, reach)[0:classes]
+    whole = jnp.concatenate([wide_rows("offset", 0, 8), wide_rows("offset", 8, 8)], axis=1)
+    turn = lax.rem(2 * channels - r * size, 2 * channels)
+    embed_offset[...] = pltpu.roll(whole, turn, 1)[0, 0:size]
+    for cp in moves[2:]:
         cp.wait()
 
 
-def finish_call(res, gx, gw1, gw2, go, gv, ge, gc, geo):
-    channels = go.shape[0]
+def finish_call(low, wide, pixels, classes):
+    channels = low.shape[1]
     rows = channels // 4
     vm = pl.BlockSpec(memory_space=pltpu.VMEM)
     hbm = pl.BlockSpec(memory_space=pl.ANY)
@@ -1132,16 +1234,21 @@
     return pl.pallas_call(
         finish_kernel,
         out_shape=(
-            out(*res.shape, kind=low_type), out(*gx.shape), line, line, kernel, line,
-            out(*ge.shape), out(2 * rows), out(*gc.shape), line, line, kernel, line, line, line,
-            out(rows, 3 * channels), out(2 * rows), out(rows, channels), line,
+            out(pixels, channels, kind=low_type), out(pixels, channels), line, line, kernel, line,
+            out(2 * rows, 2 * channels), out(2 * rows), out(classes // 4, 2 * channels), line, line,
+            kernel, line, line, line, out(rows, 3 * channels), out(2 * rows), out(rows, channels),
+            line,
         ),
-        in_specs=[hbm, hbm, vm, vm, vm, vm, hbm, hbm, vm],
-        out_specs=(hbm, hbm, vm, vm, vm, vm, hbm, vm, hbm) + (vm,) * 10,
-        scratch_shapes=[pltpu.SemaphoreType.DMA((4,))],
-        compiler_params=pltpu.CompilerParams(vmem_limit_bytes=32 << 20),
+        in_specs=[hbm] * 2,
+        out_specs=(hbm, hbm) + (vm,) * 17,
+        scratch_shapes=[
+            pltpu.VMEM(low.shape, low_type),
+            pltpu.VMEM(wide.shape, float_type),
+            pltpu.SemaphoreType.DMA((4,)),
+        ],
+        compiler_params=pltpu.CompilerParams(vmem_limit_bytes=60 << 20),
         name="finish",
-    )(res, gx, gw1, gw2, go, gv, ge, gc, geo)
+    )(low, wide)
 
 
 def shards(
@@ -1180,7 +1287,7 @@
         x, cot, lines, (level_count, level_index, labels), first_kernel, second_kernel,
         joint_weight, output_weight, embed_weight, class_table,
     )
-    outs = finish_call(*found)
+    outs = finish_call(*found, image_count * pixels, class_table.shape[0])
     return (outs[0].reshape(images.shape), outs[1].reshape(images.shape)) + tuple(outs[2:])
 
 

time: 160 us -> 145 us (0.906)
  local copies, waits for them, and re-layouts: 9.22 us -> 0 us
  Pallas kernels: 149 us -> 144 us
    unnamed x18 -> x0, local copies, waits for them, and re-layouts: 9.22 us -> none
    pallas_call x2, Pallas kernels: 149 us -> 144 us  [the longest x1 138 us: block_call(): pl.pallas_call(block_kernel, out_shape=(out(sum(low_at['jo']), channels,...]
where the time goes in v1:
time: 145 us
  Pallas kernels  144 us (99%)
    pallas_call x1, Pallas kernels, block_call(): pl.pallas_call(block_kernel, out_shape=(out(sum(low_at['jo']), channels,...  138 us
    pallas_call x1, Pallas kernels, finish_call(): pl.pallas_call(finish_kernel, out_shape=(out(pixels, channels, kind=low_t...  5.66 us

profile of v1, /device:TPU:0, one launch (start us, length us, event | category | flops | bytes accessed | tf_op | source)
XLA Modules:
  0.0 144.7 jit_solution(7858508165809654449)
XLA Ops:
  0.7 138.2 %block.1 = (bf16[2944,384]{1,0:T(8,128)(2,1)}, f32[1712,384]{1,0:T(8,128)}) custom-call(bf16[3,256,384]{2,1,0:T(8,128)(2,1)} %bitcast.4, bf16[3,256,384]{2,1,0:T(8,128)(2,1)} %bitcast.5, bf16[384]{0:T(512)(128)(2,1)} %rest_0_.1, bf16[384]{0:T(512)(128)(2,1)} %rest_1_.1, bf16[384]{0:T(512)(128)(2,1)} %rest_2_.1, bf16[384]{0:T(512)(128)(2,1)} %rest_3_.1, ...), custom_call_target="tpu_custom_call" | custom-call | tf_op jit(solution)/shard_map/block/pallas_call | solution.py:1116
  138.8 5.7 %finish.1 = (bf16[768,384]{1,0:T(8,128)(2,1)}, f32[768,384]{1,0:T(8,128)}, f32[96]{0:T(128)}, f32[96]{0:T(128)}, f32[864,384]{1,0:T(8,128)}, /*index=5*/f32[96]{...) custom-call(bf16[2944,384]{1,0:T(8,128)(2,1)} %get-tuple-element.40., ...), custom_call_target="tpu_custom_call" | custom-call | tf_op jit(solution)/shard_map/finish/pallas_call | solution.py:1234

commit v2 on v1

--- a/solution.py
+++ b/solution.py
@@ -77,27 +77,42 @@
     size = lax.axis_size("img")
     z = lax.rem(lax.div(i, 2), 4)
     e = lax.div(i, 8)
+    y = lax.rem(i, 2)
     others = (z + 1 - 2 * lax.rem(z, 2), lax.rem(z + 2, 4), 3 - z)
     more = size // 8
+    near = [(i + 2 * (n - z), r) for n in others]
+    over = [(i + 1 - 2 * y + 2 * (n - z), r) for n in others]
+    aside = [(i + 1 - 2 * y, r)]
     return {
-        "y": [(i + 1 - 2 * lax.rem(i, 2), r)],
-        "z": [(i + 2 * (n - z), r) for n in others],
+        "y": aside,
+        "z": near,
+        "all": near + aside + over,
         "e": [(i + 8 * (lax.rem(e + k, more) - e), r) for k in range(1, more)],
-        "at": (lax.rem(i, 2), z),
+        "at": (y, z),
         "pieces": others,
+        "places": [(y, n) for n in others] + [(1 - y, z)] + [(1 - y, n) for n in others],
     }
 
 
 class Reduction:
-    def __init__(self, out, lanes, n, q, refs, who, place, cs, cr, es, er):
-        if n is not None:
-            refs = (refs[0].at[n],) + tuple(ref.at[n] for ref in refs[1:])
-        self.grad, self.got_core, self.got_x, self.own, self.got_y, self.got_z, self.got_e = refs
-        self.out, self.lanes, self.q, self.who = out, lanes, q, who
+    def __init__(self, out, start, size, mode, q, refs, who, place, cs, cr, es, er):
+        def cut(ref, part):
+            lead = (slice(None),) * (len(ref.shape) - 2)
+            return ref.at[lead + (pl.ds(start // part, size // part),)]
+
+        grad, core, got_x, own, got_y, got_z, got_e, two, every = refs
+        self.grad, self.got_core, self.got_x = cut(grad, 1), cut(core, 1), cut(got_x, 1)
+        self.own, self.got_y = cut(own, 2), cut(got_y, 2)
+        self.got_z, self.got_e = cut(got_z, 8), cut(got_e, 8)
+        self.got_two, self.got_all = two, every
+        self.out = out.at[pl.ds(start, size)]
+        self.mode, self.q, self.who, self.size = mode, q, who, size
         self.c, self.x, self.chips = place
         self.y, self.z = self.chips["at"]
         self.sems = (cs, cr, es, er)
-        self.size = self.got_x.shape[0]
+        self.near, self.far = 2 * self.x + self.c, 2 * (1 - self.x) + self.c
+        self.low, self.high = lax.rem(self.z, 2), lax.div(self.z, 2)
+        self.slot = 2 * self.low + self.high if mode == "h" else self.z
 
     def copy(self, src, dst, n, at, extra=False):
         send, recv = self.sems[2:] if extra else self.sems[:2]
@@ -120,98 +135,214 @@
         ]
 
     def x_copies(self):
-        return [self.copy(self.grad.at[2 * (1 - self.x) + self.c], self.got_x, 2, self.who[2])]
+        if self.mode == "y":
+            rows = self.half(self.y)
+            return [self.copy(self.grad.at[self.far, rows], self.got_x.at[rows], 2, self.who[2])]
+        return [self.copy(self.grad.at[self.far], self.got_x, 2, self.who[2])]
 
     def y_copies(self):
-        return [self.copy(self.got_x.at[self.half(1 - self.y)], self.got_y, 3, self.chips["y"][0])]
+        rows, at = self.half(1 - self.y), self.chips["y"][0]
+        if self.mode == "y":
+            return [
+                self.copy(self.grad.at[2 * n + self.c, rows], self.got_two.at[n], 3 + n, at)
+                for n in range(2)
+            ]
+        return [self.copy(self.got_x.at[rows], self.got_y, 3, at)]
+
+    def first_z_copies(self):
+        return [
+            self.copy(
+                self.got_x.at[self.piece(2 * (1 - self.low) + n, self.y)], self.got_z.at[n], 5 + n,
+                self.chips["z"][0],
+            )
+            for n in range(2)
+        ]
+
+    def second_z_copies(self):
+        part = self.got_x.at[self.piece(2 * self.low + 1 - self.high, self.y)]
+        return [self.copy(part, self.got_z.at[2], 7, self.chips["z"][1])]
+
+    def back_second_copies(self):
+        part = self.out.at[self.piece(self.slot, self.y)]
+        return [self.copy(part, part, 8, self.chips["z"][1])]
+
+    def back_first_copies(self):
+        part = self.out.at[self.quarter()]
+        return [self.copy(part, part, 9, self.chips["z"][0])]
+
+    def quarter(self, y=None):
+        size = self.size // 4
+        y = self.y if y is None else y
+        return pl.ds(pl.multiple_of(y * (self.size // 2) + self.low * size, size), size)
 
     def z_copies(self):
         return [
-            self.copy(self.got_x.at[self.piece(p, self.y)], self.got_z.at[n], 4 + n, at)
+            self.copy(self.got_x.at[self.piece(p, self.y)], self.got_z.at[n], 5 + n, at)
             for n, (p, at) in enumerate(zip(self.chips["pieces"], self.chips["z"]))
         ]
 
+    def spread_copies(self):
+        return [
+            self.copy(self.got_x.at[self.piece(z, y)], self.got_all.at[n], 12 + n, at)
+            for n, ((y, z), at) in enumerate(zip(self.chips["places"], self.chips["all"]))
+        ]
+
     def extra_copies(self):
-        src = self.got_x.at[self.piece(self.z, self.y)]
+        src = self.got_x.at[self.piece(self.slot, self.y)]
         return [
             self.copy(src, self.got_e.at[n], n, at, True) for n, at in enumerate(self.chips["e"])
         ]
 
     def back_z_copies(self):
-        part = self.out.at[self.piece(self.z, self.y), self.lanes]
-        return [self.copy(part, part, 7 + n, at) for n, at in enumerate(self.chips["z"])]
+        part = self.out.at[self.piece(self.z, self.y)]
+        return [self.copy(part, part, 8 + n, at) for n, at in enumerate(self.chips["z"])]
 
     def back_y_copies(self):
-        part = self.out.at[self.half(self.y), self.lanes]
-        return [self.copy(part, part, 10, self.chips["y"][0])]
+        part = self.out.at[self.half(self.y)]
+        return [self.copy(part, part, 11, self.chips["y"][0])]
+
+    def back_copies(self):
+        part = self.out.at[self.piece(self.z, self.y)]
+        return [self.copy(part, part, 19 + n, at) for n, at in enumerate(self.chips["all"])]
+
+    @staticmethod
+    def start(copies):
+        for cp in copies:
+            cp.start()
+
+    @staticmethod
+    def arrived(copies):
+        for cp in copies:
+            cp.wait_recv()
 
     def core(self):
-        for cp in self.core_copies():
-            cp.start()
+        self.start(self.core_copies())
+
+    def pair_sum(self, n, *rows):
+        return self.grad[(2 * n + self.c, *rows)].astype(float_type) + self.got_core[
+            (n, *rows)
+        ].astype(float_type)
+
+    def chip_sum(self, rows):
+        return self.pair_sum(self.x, rows) + self.got_x[rows].astype(float_type)
 
     def across_x(self):
-        for cp in self.core_copies():
-            cp.wait_recv()
-        far = 1 - self.x
-        block = 2 * far + self.c
-        self.grad[block] = (
-            self.grad[block].astype(float_type) + self.got_core[far].astype(float_type)
-        ).astype(low_type)
-        self.x_copies()[0].start()
-
-    def chip_sum(self, rows):
-        return (
-            self.grad[2 * self.x + self.c, rows].astype(float_type)
-            + self.got_core[self.x, rows].astype(float_type)
-            + self.got_x[rows].astype(float_type)
-        )
+        if self.mode == "y":
+            self.arrived(self.y_copies())
+            rows = self.half(self.y)
+            for n, far in ((1 - self.x, True), (self.x, False)):
+                v = self.pair_sum(n, rows) + self.got_two[n].astype(float_type)
+                if far:
+                    self.grad[self.far, rows] = v.astype(low_type)
+                    self.start(self.x_copies())
+                else:
+                    self.own[...] = v
+            return
+        self.arrived(self.core_copies())
+        self.grad[self.far] = self.pair_sum(1 - self.x).astype(low_type)
+        self.start(self.x_copies())
 
     def across_y(self):
-        self.x_copies()[0].wait_recv()
         rows = self.half(1 - self.y)
+        if self.mode == "y":
+            self.arrived(self.core_copies())
+            for n in range(2):
+                self.grad[2 * n + self.c, rows] = self.pair_sum(n, rows).astype(low_type)
+            self.start(self.y_copies())
+            return
+        self.arrived(self.x_copies())
         self.got_x[rows] = self.chip_sum(rows).astype(low_type)
-        self.y_copies()[0].start()
+        self.start(self.y_copies())
         self.own[...] = self.chip_sum(self.half(self.y))
 
     def across_z(self):
-        self.y_copies()[0].wait_recv()
-        v = self.own[...] + self.got_y[...].astype(float_type)
+        rows = self.half(self.y)
+        if self.mode == "y":
+            self.arrived(self.x_copies())
+            v = self.own[...] + self.got_x[rows].astype(float_type)
+        else:
+            self.arrived(self.y_copies())
+            v = self.own[...] + self.got_y[...].astype(float_type)
         self.own[...] = v
-        self.got_x[self.half(self.y)] = v.astype(low_type)
-        for cp in self.z_copies():
-            cp.start()
+        self.got_x[rows] = v.astype(low_type)
+        self.start(self.first_z_copies() if self.mode == "h" else self.z_copies())
+
+    def second_z(self):
+        self.arrived(self.first_z_copies())
+        for n in range(2):
+            rows = self.piece(2 * self.low + n)
+            v = self.own[rows] + self.got_z[n].astype(float_type)
+            self.own[rows] = v
+            self.got_x[self.piece(2 * self.low + n, self.y)] = v.astype(low_type)
+        self.start(self.second_z_copies())
+
+    def second_back(self):
+        self.arrived(self.back_second_copies())
+        self.start(self.back_first_copies())
+
+    def finish(self, v):
+        if self.chips["e"]:
+            self.got_x[self.piece(self.slot, self.y)] = v.astype(low_type)
+            self.start(self.extra_copies())
+            for n, cp in enumerate(self.extra_copies()):
+                cp.wait_recv()
+                v = v + self.got_e[n].astype(float_type)
+        self.out[self.piece(self.slot, self.y)] = v.astype(low_type)
 
     def back_z(self):
-        for cp in self.z_copies():
-            cp.wait_recv()
+        if self.mode == "h":
+            self.arrived(self.second_z_copies())
+            self.finish(self.own[self.piece(self.slot)] + self.got_z[2].astype(float_type))
+            self.start(self.back_second_copies())
+            return
+        self.arrived(self.z_copies())
         v = self.own[self.piece(self.z)]
         for n in range(3):
             v = v + self.got_z[n].astype(float_type)
-        if self.chips["e"]:
-            self.got_x[self.piece(self.z, self.y)] = v.astype(low_type)
-            for cp in self.extra_copies():
-                cp.start()
-            for n, cp in enumerate(self.extra_copies()):
-                cp.wait_recv()
-                v = v + self.got_e[n].astype(float_type)
-        self.out[self.piece(self.z, self.y), self.lanes] = v.astype(low_type)
-        for cp in self.back_z_copies():
-            cp.start()
+        self.finish(v)
+        self.start(self.back_z_copies())
+
+    def spread(self):
+        self.arrived(self.x_copies())
+        size = self.size // 8
+        self.own[0:size] = self.chip_sum(self.piece(self.z, self.y))
+        for y in range(2):
+            rows = self.half(y)
+            self.got_x[rows] = self.chip_sum(rows).astype(low_type)
+        self.start(self.spread_copies())
+
+    def back(self):
+        self.arrived(self.spread_copies())
+        v = self.own[0 : self.size // 8]
+        for n in range(7):
+            v = v + self.got_all[n].astype(float_type)
+        self.finish(v)
+        self.start(self.back_copies())
 
     def back_y(self):
-        for cp in self.back_z_copies():
-            cp.wait_recv()
-        self.back_y_copies()[0].start()
+        self.arrived(self.back_first_copies() if self.mode == "h" else self.back_z_copies())
+        self.start(self.back_y_copies())
 
     def end(self):
-        self.back_y_copies()[0].wait_recv()
+        self.arrived(self.back_copies() if self.mode == "all" else self.back_y_copies())
 
     def drain(self):
-        for cp in (
-            self.core_copies() + self.x_copies() + self.y_copies() + self.z_copies()
-            + self.extra_copies() + self.back_z_copies() + self.back_y_copies()
-        ):
+        sent = self.core_copies() + self.x_copies() + self.extra_copies()
+        if self.mode == "all":
+            sent += self.spread_copies() + self.back_copies()
+        elif self.mode == "h":
+            sent += self.y_copies() + self.first_z_copies() + self.second_z_copies()
+            sent += self.back_second_copies() + self.back_first_copies() + self.back_y_copies()
+        else:
+            sent += (
+                self.y_copies() + self.z_copies() + self.back_z_copies() + self.back_y_copies()
+            )
+        for cp in sent:
             cp.wait_send()
+
+
+CHUNKS2 = ((384, "x"), (256, "x"), (256, "x"))
+CHUNKS1 = ((384, "x"), (256, "x"), (256, "x"))
 
 
 def out_rows(pixels, channels, classes):
@@ -233,21 +364,25 @@
 
 
 def block_kernel(
-    x_ref, cot_ref, *rest,
+    *rest,
 ):
-    lines, rest = rest[:11], rest[11:]
-    count_ref, index_ref, label_ref = rest[:3]
+    small_any, rest = rest[:16], rest[16:]
     (w1_any, w2_any, jw_any, ow_any, ew_any, ct_any,
-    low_out, wide_out,
+    low_any, wide_any,
     w1, w2, jw, ow, ew, ct, ones, hid, mid, mod, emb, act1_t, act2_t, st, m1, m3, got,
     att, att_t, kv, kv_t, q8, d_out_t, qm, dom, s_ref, eb, dsb, mix_t, dq_t, dq, dkv,
     got_core, to_x, got_x, ag, q_sum, kv_sum, o_sum, gjo,
     grad, slope_grad, gs, mg,
-    gw, w_core, w_got_x, w_own, w_got_y, w_got_z, w_got_e,
+    gw, w_core, w_got_x, w_own, w_got_y, w_got_z, w_got_e, got_two, got_all,
     o_core, o_got_x, o_own, o_got_y, o_got_z, o_got_e,
     v_own, v_row, v_one, v_y, v_two, v_z, v_three, v_e, g_row, gat, left, hot,
     vec_ref, prep_ref, wsem, ssem, rsem, gsend, grecv, asem, bsem, cs, cr, es, er, vs, vr, gsem,
-    hsem) = rest[3:]
+    hsem, low_out, wide_out, osem, isem, x_ref, cot_ref, *held) = rest
+    lines, (count_ref, index_ref, label_ref) = held[:11], held[11:]
+    enter = [
+        pltpu.make_async_copy(src, dst, isem.at[n])
+        for n, (src, dst) in enumerate(zip(small_any, (x_ref, cot_ref, *held)))
+    ]
     images, pixels, channels = x_ref.shape
     width = 32
     edge = pixels - width
@@ -268,6 +403,10 @@
     inner_halo = pl.multiple_of((pixels + width) * (1 - c), width)
     outer_halo = pl.multiple_of((pixels + width) * c, width)
     outer_live = jnp.logical_and(r > 0, r < 3)
+    barrier = pltpu.get_barrier_semaphore()
+    greeted = list(who.values()) + chips["all"] + chips["e"]
+    for at in greeted:
+        pl.semaphore_signal(barrier, inc=1, device_id=at, device_id_type=MESH)
     loads = {
         name: pltpu.make_async_copy(src, dst, wsem.at[n])
         for n, (name, src, dst) in enumerate((
@@ -275,12 +414,8 @@
             ("jw", jw_any, jw), ("ow", ow_any, ow),
         ))
     }
-    for cp in loads.values():
+    for cp in enter + list(loads.values()):
         cp.start()
-    barrier = pltpu.get_barrier_semaphore()
-    greeted = list(who.values()) + chips["y"] + chips["z"] + chips["e"]
-    for at in greeted:
-        pl.semaphore_signal(barrier, inc=1, device_id=at, device_id_type=MESH)
 
     abuf = grad.at[0]
     low_at, wide_at = out_rows(images * pixels, channels, ct.shape[0])
@@ -392,41 +527,49 @@
                 total = more if total is None else total + more
         return total
 
-    def kernel_grad(act_t, buf, base):
+    def kernel_grad(act_t, buf, base, first, last):
         for dy in range(3):
             for dx in range(3):
                 tap = 3 * dy + dx
                 at = (2 - dx) * channels
                 g = None
-                for b in range(images):
+                for b in range(first, last):
                     more = dot(
                         act_t[:, b * pixels : (b + 1) * pixels],
                         buf[b, (2 - dy) * width : (2 - dy) * width + pixels, at : at + channels],
                     )
                     g = more if g is None else g + more
-                g = g.astype(low_type)
                 for m in range(4):
                     lo = max(tap * channels, m * quarter)
                     hi = min((tap + 1) * channels, (m + 1) * quarter)
-                    for n in range(3 if lo < hi else 0):
-                        gw[base + n, m, lo - m * quarter : hi - m * quarter] = g[
-                            lo - tap * channels : hi - tap * channels, 128 * n : 128 * n + 128
-                        ]
-
-    def reduction(out, lanes, n, q, refs):
-        return Reduction(out, lanes, n, q, refs, who, place, cs, cr, es, er)
-
-    refs = (gw, w_core, w_got_x, w_own, w_got_y, w_got_z, w_got_e)
-    red2 = [reduction(gw2_ref, slice(128 * n, 128 * n + 128), n, n, refs) for n in range(3)]
-    red1 = [reduction(gw1_ref, slice(128 * n, 128 * n + 128), n + 3, n + 3, refs) for n in range(3)]
-    refs = (gjo, o_core, o_got_x, o_own, o_got_y, o_got_z, o_got_e)
-    red0 = reduction(go_ref, slice(0, channels), None, 6, refs)
+                    if lo < hi:
+                        v = g[lo - tap * channels : hi - tap * channels]
+                        rows = slice(lo - m * quarter, hi - m * quarter)
+                        if first > 0:
+                            v = v + gw[base, m, rows].astype(float_type)
+                        gw[base, m, rows] = v.astype(low_type)
+
+    def reduction(out, start, size, mode, q, refs):
+        return Reduction(out, start, size, mode, q, refs, who, place, cs, cr, es, er)
+
+    def reductions(n, out, first, sizes):
+        refs = tuple(ref.at[n] for ref in (gw, w_core, w_got_x, w_own, w_got_y, w_got_z, w_got_e))
+        found, at = [], 0
+        for q, (size, mode) in enumerate(sizes):
+            found.append(reduction(out, at, size, mode, first + q, refs + (got_two, got_all)))
+            at += size
+        return found
+
+    red2 = reductions(1, gw2_ref, 0, CHUNKS2)
+    red1 = reductions(0, gw1_ref, 4, CHUNKS1)
+    refs = (gjo, o_core, o_got_x, o_own, o_got_y, o_got_z, o_got_e, got_two, got_all)
+    red0 = reduction(go_ref, 0, channels, "x", 8, refs)
     zs, extras = chips["z"], chips["e"]
 
     def small_row_copies(s):
         return [
             remote(v_own.at[s], v_row.at[s, k - 1], vs.at[s, k - 1], vr.at[s, k - 1], who[k])
-            for k in (1, 2, 3)
+            for k in (1, 2)
         ]
 
     def small_y_copies(s):
@@ -446,19 +589,24 @@
 
     def small_row(s):
         v_own[s] = gs[...]
-        start(small_row_copies(s))
+        start(small_row_copies(s)[:1])
+
+    def small_x(s):
+        small_row_copies(s)[0].wait_send()
+        small_row_copies(s)[0].wait_recv()
+        v_own[s] = v_own[s] + v_row[s, 0]
+        start(small_row_copies(s)[1:])
 
     def small_y(s):
-        arrived(small_row_copies(s))
-        v = v_own[s] + v_row[s, 0] + v_row[s, 1] + v_row[s, 2]
+        arrived(small_row_copies(s)[1:])
+        v = v_own[s] + v_row[s, 1]
         quarter_of = channels // 4
         v = pltpu.roll(v, lax.rem(channels - r * quarter_of, channels), 1)
         v_one[s] = v[:, 0:128]
         if s == 0:
             double = lax.rem(r, 2) * 2 * quarter_of
-            pair = jnp.where(r < 2, v_own[0, 8:9], v_own[0, 9:10])
-            for k in range(3):
-                pair = pair + jnp.where(r < 2, v_row[0, k, 8:9], v_row[0, k, 9:10])
+            pair = v_own[0, 8:10] + v_row[0, 1, 8:10]
+            pair = jnp.where(r < 2, pair[0:1], pair[1:2])
             pair = pltpu.roll(pair, lax.rem(channels - double, channels), 1)
             v_one[0, 8:9] = pair[:, 0:128]
             v_one[0, 9:10] = pltpu.roll(pair, channels - 128, 1)[:, 0:128]
@@ -483,7 +631,7 @@
     def gather_row_copies():
         return [
             remote(mg, g_row.at[k - 1], gsem.at[k - 1], hsem.at[k - 1], who[k])
-            for k in (1, 2, 3)
+            for k in (1, 2)
         ]
 
     def gather_copies():
@@ -502,11 +650,17 @@
         return [remote(gat.at[c], gat.at[c], gsem.at[n], hsem.at[n], who[1])]
 
     def gather_row():
-        start(gather_row_copies())
+        start(gather_row_copies()[:1])
+
+    def gather_x():
+        gather_row_copies()[0].wait_send()
+        gather_row_copies()[0].wait_recv()
+        mg[...] = mg[...] + g_row[0]
+        start(gather_row_copies()[1:])
 
     def gather_y():
-        arrived(gather_row_copies())
-        v = emb[...] + mg[...] + g_row[0] + g_row[1] + g_row[2]
+        arrived(gather_row_copies()[1:])
+        v = emb[...] + mg[...] + g_row[1]
         gat[c, i] = jnp.where(c == 0, v[:, :channels], v[:, channels:])
         start(gather_copies()[:1])
 
@@ -613,6 +767,24 @@
             marks = jnp.where(here, label_ref[b].astype(float_type), marks)
         emb[...] = rows + marks
 
+    leaving = []
+
+    def leave(src, dst, first, size):
+        rows = pl.ds(first, size)
+        cp = pltpu.make_async_copy(src.at[rows], dst.at[rows], osem.at[len(leaving)])
+        cp.start()
+        leaving.append(cp)
+
+    def leave_low(name, first=0, size=None):
+        at, rows = low_at[name]
+        leave(low_out, low_any, at + first, size or rows)
+
+    def leave_wide(name, last=None):
+        at, rows = wide_at[name]
+        leave(wide_out, wide_any, at, sum(wide_at[last or name]) - at)
+
+    for cp in enter:
+        cp.wait()
     at = 0
     for line in lines:
         v = line[...].astype(float_type).reshape(1, line.shape[0])
@@ -623,12 +795,9 @@
     gs[...] = jnp.zeros(gs.shape, float_type)
     mg[...] = jnp.zeros(mg.shape, float_type)
 
-    def clear(n, _):
+    for n in range(2):
         for m in range(4):
-            gw[n, m, quarter:padded] = jnp.zeros((padded - quarter, 128), low_type)
-        return 0
-
-    lax.fori_loop(0, 6, clear, 0)
+            gw[n, m, quarter:padded] = jnp.zeros((padded - quarter, channels), low_type)
 
     @each_image
     def _(b):
@@ -827,44 +996,66 @@
             lanes = pl.ds(pl.multiple_of(t * pair_lanes, pair_lanes), pair_lanes)
             v_lanes = pl.ds(pl.multiple_of(channels + t * pair_lanes, pair_lanes), pair_lanes)
             qm[...] = masked(q8[:, lanes].astype(float_type))
-            peak = None
-            for n in range(whole // chunk):
-                rows = pl.ds(n * chunk, chunk)
-                s = dot_nt(kv[rows, lanes], qm[...])
-                s_ref[rows] = s
-                top = jnp.max(s.reshape(chunk // 8, 8, 2 * pixels), axis=0)
-                peak = top if peak is None else jnp.maximum(peak, top)
-            peak = jnp.max(peak, axis=0, keepdims=True)
-            total = None
-            for n in range(whole // chunk):
-                rows = pl.ds(n * chunk, chunk)
-                e = jnp.exp(s_ref[rows] - peak)
-                eb[rows] = e.astype(low_type)
-                more = jnp.sum(e.reshape(chunk // 8, 8, 2 * pixels), axis=0)
-                total = more if total is None else total + more
-            over = 1.0 / jnp.sum(total, axis=0, keepdims=True)
-            inner_of, scaled = [], []
-            for j in range(2):
-                head = pl.ds(pl.multiple_of(t * pair_lanes + j * HEAD, HEAD), HEAD)
-                v_head = pl.ds(pl.multiple_of(channels + t * pair_lanes + j * HEAD, HEAD), HEAD)
-                cols = slice(j * pixels, (j + 1) * pixels)
-                mt = dot(kv_t[v_head, :], eb[:, cols]) * over[:, cols]
-                mix_t[head] = mt.astype(low_type)
-                g = (d_out_t[b, head].astype(float_type) * over[:, cols]).astype(low_type).astype(float_type)
-                inner_of.append(col_sum(g * mt))
-                scaled.append(g)
-            inner_of = jnp.concatenate(inner_of, axis=1)
-            dom[...] = masked(jnp.concatenate(scaled, axis=0).T)
-            for n in range(whole // chunk):
-                rows = pl.ds(n * chunk, chunk)
-                dp = dot_nt(kv[rows, v_lanes], dom[...])
-                dsb[rows] = (eb[rows].astype(float_type) * (dp - inner_of)).astype(low_type)
-            for j in range(2):
-                head = pl.ds(pl.multiple_of(t * pair_lanes + j * HEAD, HEAD), HEAD)
-                cols = slice(j * pixels, (j + 1) * pixels)
-                dq_t[head] = dot(kv_t[head, :], dsb[:, cols]) * HEAD ** (-0.5)
+            rows_of = [pl.ds(n * chunk, chunk) for n in range(whole // chunk)]
+            cols_of = [slice(j * pixels, (j + 1) * pixels) for j in range(2)]
+            head_of = [
+                pl.ds(pl.multiple_of(t * pair_lanes + j * HEAD, HEAD), HEAD) for j in range(2)
+            ]
+            value_of = [
+                pl.ds(pl.multiple_of(channels + t * pair_lanes + j * HEAD, HEAD), HEAD)
+                for j in range(2)
+            ]
+
+            def score(j, rows, peak):
+                s = dot_nt(kv[rows, lanes], qm[cols_of[j], :])
+                s_ref[rows, cols_of[j]] = s
+                top = jnp.max(s.reshape(chunk // 8, 8, pixels), axis=0)
+                return top if peak is None else jnp.maximum(peak, top)
+
+            def raise_to(j, rows, peak, total):
+                e = jnp.exp(s_ref[rows, cols_of[j]] - peak)
+                eb[rows, cols_of[j]] = e.astype(low_type)
+                more = jnp.sum(e.reshape(chunk // 8, 8, pixels), axis=0)
+                return more if total is None else total + more
+
+            def mix(j, total):
+                over = 1.0 / col_sum(total)
+                mt = dot(kv_t[value_of[j], :], eb[:, cols_of[j]]) * over
+                mix_t[head_of[j]] = mt.astype(low_type)
+                g = (d_out_t[b, head_of[j]].astype(float_type) * over).astype(low_type)
+                g = g.astype(float_type)
+                none = jnp.zeros_like(g)
+                both = jnp.concatenate([g, none] if j == 0 else [none, g], axis=0)
+                dom[cols_of[j], :] = both.T.astype(low_type)
+                return col_sum(g * mt)
+
+            def score_back(j, rows, inner_of):
+                dp = dot_nt(kv[rows, v_lanes], dom[cols_of[j], :])
+                e = eb[rows, cols_of[j]].astype(float_type)
+                dsb[rows, cols_of[j]] = (e * (dp - inner_of)).astype(low_type)
+
+            def query_back(j):
+                dq_t[head_of[j]] = dot(kv_t[head_of[j], :], dsb[:, cols_of[j]]) * HEAD ** (-0.5)
+
+            peak0 = peak1 = total0 = total1 = None
+            for rows in rows_of:
+                peak0 = score(0, rows, peak0)
+            peak0 = jnp.max(peak0, axis=0, keepdims=True)
+            for rows in rows_of:
+                peak1 = score(1, rows, peak1)
+                total0 = raise_to(0, rows, peak0, total0)
+            peak1 = jnp.max(peak1, axis=0, keepdims=True)
+            inner0 = mix(0, total0)
+            for rows in rows_of:
+                score_back(0, rows, inner0)
+                total1 = raise_to(1, rows, peak1, total1)
+            inner1 = mix(1, total1)
+            query_back(0)
+            for rows in rows_of:
+                score_back(1, rows, inner1)
+            dkv[:, v_lanes] = dot(eb[...], dom[...]).astype(low_type)
+            query_back(1)
             dkv[:, lanes] = dot(dsb[...], qm[...]).astype(low_type)
-            dkv[:, v_lanes] = dot(eb[...], dom[...]).astype(low_type)
             return 0
 
         lax.fori_loop(0, pairs, one_pair, 0)
@@ -895,12 +1086,12 @@
         q_sum[...] += dot(att_t[:, span_of(r)], dq[...])
         kv_sum[...] += dot(att_t[...], dkv[...])
 
+        o_sum[...] += dot(mix_t[...], cot_ref[b])
+        low_out[span_of(b)] = mix_t[...].T
+
         @pl.when(b == images - 1)
         def _():
             pass_on(b)
-
-        o_sum[...] += dot(mix_t[...], cot_ref[b])
-        low_out[span_of(b)] = mix_t[...].T
 
     def pack_weights():
         part_rows = channels // 4
@@ -993,83 +1184,100 @@
         v = scaled * (slope_grad[b] * vec(0) - first - normed * second)
         wide_out[span_of(b)] = ag[b, width : width + pixels] + v
 
+    some_images(branch_grad, 0, images - 1)
     pack_weights()
-    some_images(branch_grad, 0, images - 1)
     red0.core()
+    kernel_grad(act2_t, grad, 1, 0, images - 1)
     red0.across_x()
     some_images(branch_back, 0, images - 1)
     some_images(branch_grad, images - 1, images)
+    kernel_grad(act2_t, grad, 1, images - 1, images)
+    red2[2].core()
     some_images(branch_back, images - 1, images)
+    red2[1].core()
+    red2[2].across_x()
+    red2[0].core()
+    each_image(result)
+    leave_low("result")
     small_row(0)
     gather_row()
-    kernel_grad(act2_t, grad, 0)
-    red2[0].core()
     red0.across_y()
-    red2[1].core()
-    red2[2].core()
+    some_images(hidden_grad, 0, images - 1)
+    some_images(hidden_grad, images - 1, images)
     red2[0].across_x()
-    each_image(result)
-    some_images(hidden_grad, 0, images - 1)
-    red2[2].across_x()
+    kernel_grad(act1_t, grad, 0, 0, images)
     red2[1].across_x()
-    small_y(0)
-    gather_y()
-    some_images(hidden_grad, images - 1, images)
     red0.across_z()
-    red2[0].across_y()
-    small_z(0)
-    gather_z()
-    kernel_grad(act1_t, grad, 3)
+    red1[0].core()
     red1[2].core()
-    red0.back_z()
-    red1[0].core()
-    red2[0].across_z()
     red1[2].across_x()
     red2[2].across_y()
+    red1[0].across_x()
+    red2[0].across_y()
+    red0.back_z()
+    red2[2].across_z()
     red1[1].core()
     red2[1].across_y()
-    red2[2].across_z()
+    red2[0].across_z()
     red1[1].across_x()
-    red1[0].across_x()
+    red0.back_y()
     some_images(hidden_back, images - 1, images)
-    red2[0].back_z()
     red1[2].across_y()
     red2[1].across_z()
     red2[2].back_z()
+    small_x(0)
+    gather_x()
     some_images(hidden_back, 0, images - 1)
+    small_row(1)
+    red2[0].back_z()
+    red1[2].across_z()
+    red2[1].back_z()
+    red1[0].across_y()
+    red1[0].across_z()
+    small_x(1)
     red1[1].across_y()
+    red2[2].back_y()
+    small_y(0)
+    gather_y()
+    red1[2].back_z()
+    red1[1].across_z()
+    red2[0].back_y()
+    red1[0].back_z()
+    red0.end()
+    leave_low("jo")
+    small_y(1)
+    red1[2].back_y()
+    red2[1].back_y()
+    red1[1].back_z()
+    red2[0].end()
+    leave_low("w2", 0, red2[0].size)
+    small_z(0)
+    gather_z()
+    red1[0].back_y()
+    small_z(1)
+    red2[2].end()
+    leave_low("w2", 640, red2[2].size)
+    each_image(images_grad)
+    leave_wide("images")
+    red1[1].back_y()
     small_end(0)
     gather_end()
-    red1[2].across_z()
-    red2[0].back_y()
-    red2[1].back_z()
-    red1[0].across_y()
-    red0.back_y()
-    red1[1].across_z()
-    small_row(1)
-    red2[2].back_y()
-    each_image(images_grad)
-    red2[0].end()
-    red1[2].back_z()
-    red1[0].across_z()
-    red1[1].back_z()
-    red1[2].back_y()
     gather_core()
     embedding()
-    red1[0].back_z()
-    red2[1].back_y()
-    small_y(1)
-    red1[1].back_y()
-    red1[0].back_y()
-    red2[2].end()
-    red0.end()
+    leave_wide("embed", "offset")
     red1[2].end()
-    small_z(1)
+    leave_low("w1", 640, red1[2].size)
+    red1[0].end()
+    leave_low("w1", 0, red1[0].size)
     small_end(1)
+    leave_wide("lines")
+    red2[1].end()
+    leave_low("w2", 384, red2[1].size)
     red1[1].end()
-    red2[1].end()
-    red1[0].end()
-
+    leave_low("w1", 384, red1[1].size)
+
+    for cp in leaving:
+        cp.wait()
     @each_image
     def _(b):
         sent = sums_core(b)
@@ -1083,9 +1291,9 @@
     for red in [red0] + red1 + red2:
         red.drain()
     for s in range(2):
-        for cp in small_row_copies(s) + small_y_copies(s) + small_z_copies(s) + small_e_copies(s):
+        for cp in small_row_copies(s)[1:] + small_y_copies(s) + small_z_copies(s) + small_e_copies(s):
             cp.wait_send()
-    for cp in gather_row_copies() + gather_copies() + gather_core_copies():
+    for cp in gather_row_copies()[1:] + gather_copies() + gather_core_copies():
         cp.wait_send()
 
 
@@ -1098,7 +1306,6 @@
     more = every // 8
     some = max(more - 1, 1)
     low_at, wide_at = out_rows(images * pixels, channels, ct.shape[0])
-    vm = pl.BlockSpec(memory_space=pltpu.VMEM)
     hbm = pl.BlockSpec(memory_space=pl.ANY)
 
     def low(*shape):
@@ -1118,8 +1325,8 @@
         out_shape=(
             out(sum(low_at["jo"]), channels, kind=low_type), out(sum(wide_at["offset"]), channels),
         ),
-        in_specs=[vm] * (2 + len(lines)) + [pl.BlockSpec(memory_space=pltpu.SMEM)] * 3 + [hbm] * 6,
-        out_specs=(vm,) * 2,
+        in_specs=[hbm] * (2 + len(lines) + 3 + 6),
+        out_specs=(hbm,) * 2,
         scratch_shapes=[
             low(*w1.shape), low(*w2.shape), low(*jw.shape), low(*ow.shape), low(*ew.shape),
             low(*ct.shape), low(channels, channels), wide(*x.shape), wide(*x.shape),
@@ -1137,20 +1344,25 @@
             wide(channels + 16, channels),
             wide(channels + 16, 2 * channels), wide(channels, channels), low(4, channels, channels),
             low(images, span, 3 * channels), wide(*x.shape), wide(16, channels), wide(8, 2 * channels),
-            low(6, 4, padded, 128), low(6, 2, padded, 128), low(6, padded, 128),
-            wide(6, padded // 2, 128), low(6, padded // 2, 128), low(6, 3, padded // 8, 128),
-            low(6, some, padded // 8, 128),
+            low(2, 4, padded, channels), low(2, 2, padded, channels), low(2, padded, channels),
+            wide(2, padded // 2, channels), low(2, padded // 2, channels),
+            low(2, 3, padded // 8, channels), low(2, some, padded // 8, channels),
+            low(2, 128, channels), low(7, 16, channels),
             low(2, channels, channels), low(channels, channels), wide(channels // 2, channels),
             low(channels // 2, channels), low(3, channels // 8, channels),
             low(some, channels // 8, channels),
-            wide(2, 16, channels), wide(2, 3, 16, channels), wide(2, 16, 128),
+            wide(2, 16, channels), wide(2, 2, 16, channels), wide(2, 16, 128),
             wide(2, 16, 128), wide(2, 16, 128), wide(2, 3, 16, 128), wide(2, 16, 128),
-            wide(2, some, 16, 128), wide(3, 8, 2 * channels), wide(2, every, 8, channels),
+            wide(2, some, 16, 128), wide(2, 8, 2 * channels), wide(2, every, 8, channels),
             low(2 * channels, 192), low(256, 192), wide(16, channels), wide(8, 2 * channels),
             dma(6), dma(7, images, 3), dma(7, images, 3), dma(images, 3), dma(images, 3),
-            dma(images, 3), dma(images, 3), dma(7, 11), dma(7, 11), dma(7, some), dma(7, some),
+            dma(images, 3), dma(images, 3), dma(9, 26), dma(9, 26), dma(9, some), dma(9, some),
             dma(2, 6 + more), dma(2, 6 + more), dma(7 + more), dma(7 + more),
-        ],
+            low(sum(low_at["jo"]), channels), wide(sum(wide_at["offset"]), channels), dma(16),
+            dma(16), low(*x.shape), low(*cot.shape),
+        ]
+        + [low(*v.shape) for v in lines]
+        + [pltpu.SMEM(v.shape, jnp.int32) for v in scalars],
         compiler_params=pltpu.CompilerParams(
             collective_id=0, has_side_effects=True, vmem_limit_bytes=62 << 20
         ),
@@ -1160,24 +1372,34 @@
 
 def finish_kernel(
     low_any, wide_any,
-    result, images, first_gain, first_shift, first_kernel, first_offset, embed_weight,
-    embed_offset, class_table, second_gain, second_shift, second_kernel, second_offset,
-    third_gain, third_shift, joint_weight, joint_offset, output_weight, output_offset,
-    low_in, wide_in, sems,
+    result, images, first_gain, first_shift, first_any, first_offset, embed_any, embed_offset,
+    classes_any, second_gain, second_shift, second_any, second_offset, third_gain, third_shift,
+    joint_any, joint_offset, output_any, output_offset,
+    low_in, wide_in, first_kernel, second_kernel, joint_weight, output_weight, embed_weight,
+    class_table, sems,
 ):
     r = lax.axis_index("row")
     rows, channels = output_weight.shape
     pixels = result.shape[0]
     low_at, wide_at = out_rows(pixels, channels, 4 * class_table.shape[0])
-    moves = [
-        pltpu.make_async_copy(src, dst, sems.at[n])
-        for n, (src, dst) in enumerate((
-            (low_any, low_in), (wide_any, wide_in), (low_in.at[pl.ds(0, pixels)], result),
-            (wide_in.at[pl.ds(0, pixels)], images),
-        ))
+    used = []
+
+    def move(src, dst):
+        cp = pltpu.make_async_copy(src, dst, sems.at[len(used)])
+        cp.start()
+        used.append(cp)
+        return cp
+
+    head = pl.ds(0, pixels)
+    low_tail = pl.ds(pixels, low_in.shape[0] - pixels)
+    wide_tail = pl.ds(pixels, wide_in.shape[0] - pixels)
+    reads = [
+        move(src.at[part], dst.at[part])
+        for src, dst, part in (
+            (low_any, low_in, low_tail), (wide_any, wide_in, wide_tail),
+            (low_any, low_in, head), (wide_any, wide_in, head),
+        )
     ]
-    moves[0].start()
-    moves[1].start()
 
     def low_rows(name, start, size):
         at = low_at[name][0] + start
@@ -1187,15 +1409,30 @@
         at = wide_at[name][0] + start
         return wide_in[at : at + size]
 
-    moves[0].wait()
-    moves[2].start()
+    reads[0].wait()
     first_kernel[...] = low_rows("w1", 0, 9 * rows)
+    move(first_kernel, first_any)
     second_kernel[...] = low_rows("w2", 0, 9 * rows)
+    move(second_kernel, second_any)
     for n in range(3):
         joint_weight[:, n * channels : (n + 1) * channels] = low_rows("jo", n * rows, rows)
     output_weight[...] = low_rows("jo", 3 * rows, rows)
-    moves[1].wait()
-    moves[3].start()
+    move(joint_weight, joint_any)
+    move(output_weight, output_any)
+    reads[2].wait()
+    move(low_in.at[head], result)
+    reads[3].wait()
+    move(wide_in.at[head], images)
+    reads[1].wait()
+    size = 2 * rows
+    classes = class_table.shape[0]
+    reach = wide_at["classes"][1] // 2
+    for n in range(2):
+        cols = slice(n * channels, (n + 1) * channels)
+        embed_weight[:, cols] = wide_rows("embed", n * size, size)
+        class_table[:, cols] = wide_rows("classes", n * reach, reach)[0:classes]
+    move(embed_weight, embed_any)
+    move(class_table, classes_any)
     lines = wide_rows("lines", 0, 32)
     for n, ref in (
         (16, first_gain), (17, first_shift), (18, first_offset), (3, second_gain),
@@ -1206,17 +1443,10 @@
     joint_offset[...] = jnp.concatenate([lines[8:9, 0:128], lines[9:10, 0:128]], axis=1)[
         0, 0 : 2 * rows
     ]
-    size = 2 * rows
-    classes = class_table.shape[0]
-    reach = wide_at["classes"][1] // 2
-    for n in range(2):
-        cols = slice(n * channels, (n + 1) * channels)
-        embed_weight[:, cols] = wide_rows("embed", n * size, size)
-        class_table[:, cols] = wide_rows("classes", n * reach, reach)[0:classes]
     whole = jnp.concatenate([wide_rows("offset", 0, 8), wide_rows("offset", 8, 8)], axis=1)
     turn = lax.rem(2 * channels - r * size, 2 * channels)
     embed_offset[...] = pltpu.roll(whole, turn, 1)[0, 0:size]
-    for cp in moves[2:]:
+    for cp in used[4:]:
         cp.wait()
 
 
@@ -1240,11 +1470,16 @@
             line,
         ),
         in_specs=[hbm] * 2,
-        out_specs=(hbm, hbm) + (vm,) * 17,
+        out_specs=(hbm, hbm, vm, vm, hbm, vm, hbm, vm, hbm, vm, vm, hbm, vm, vm, vm, hbm, vm, hbm, vm),
         scratch_shapes=[
             pltpu.VMEM(low.shape, low_type),
             pltpu.VMEM(wide.shape, float_type),
-            pltpu.SemaphoreType.DMA((4,)),
+            pltpu.VMEM((9 * rows, channels), float_type),
+            pltpu.VMEM((9 * rows, channels), float_type),
+            pltpu.VMEM((rows, 3 * channels), float_type), pltpu.VMEM((rows, channels), float_type),
+            pltpu.VMEM((2 * rows, 2 * channels), float_type),
+            pltpu.VMEM((classes // 4, 2 * channels), float_type),
+            pltpu.SemaphoreType.DMA((12,)),
         ],
         compiler_params=pltpu.CompilerParams(vmem_limit_bytes=60 << 20),
         name="finish",

time: 145 us -> 143 us (0.986)
  Pallas kernels: 144 us -> 142 us
where the time goes in v2:
time: 143 us
  Pallas kernels  142 us (99%)
    pallas_call x1, Pallas kernels, block_call(): pl.pallas_call(block_kernel, out_shape=(out(sum(low_at['jo']), channels,...  137 us
    pallas_call x1, Pallas kernels, finish_call(): pl.pallas_call(finish_kernel, out_shape=(out(pixels, channels, kind=low_t...  4.93 us

profile of v2, /device:TPU:0, one launch (start us, length us, event | category | flops | bytes accessed | tf_op | source)
XLA Modules:
  0.0 142.8 jit_solution(5800534141520802551)
XLA Ops:
  0.7 137.0 %block.1 = (bf16[2944,384]{1,0:T(8,128)(2,1)}, f32[1712,384]{1,0:T(8,128)}) custom-call(bf16[3,256,384]{2,1,0:T(8,128)(2,1)} %bitcast.4, bf16[3,256,384]{2,1,0:T(8,128)(2,1)} %bitcast.5, bf16[384]{0:T(512)(128)(2,1)} %rest_2_.1, bf16[384]{0:T(512)(128)(2,1)} %rest_3_.1, bf16[384]{0:T(512)(128)(2,1)} %rest_4_.1, bf16[384]{0:T(512)(128)(2,1)} %rest_5_.1, ...), custom_call_target="tpu_custom_call" | custom-call | tf_op jit(solution)/shard_map/block/pallas_call | solution.py:1323
  137.7 4.9 %finish.1 = (bf16[768,384]{1,0:T(8,128)(2,1)}, f32[768,384]{1,0:T(8,128)}, f32[96]{0:T(128)}, f32[96]{0:T(128)}, f32[864,384]{1,0:T(8,128)}, /*index=5*/f32[96]{...) custom-call(bf16[2944,384]{1,0:T(8,128)(2,1)} %get-tuple-element.40., ...), custom_call_target="tpu_custom_call" | custom-call | tf_op jit(solution)/shard_map/finish/pallas_call | solution.py:1464
